TPU v7x, 32 devices: a whole 2x2x4 slice. The times are simulated.
32 devices in a mesh: section: 2 (over core), row: 4 (over z), col: 4 (over y, x).
Axes of the slice: x: 2, y: 2, z: 4, core: 2. Of those that a mesh axis runs over, the one named last changes fastest.
Arguments:
- inputs: bfloat16 [2, 512, 6144], P(None, 'row'), may hold values from -6 to 6
- norm_gain: float32 [2, 6144], P('section'), may hold values from 0.1 to 1.9
- w_in: bfloat16 [2, 4, 4, 64, 128, 128], P('section', 'row', 'col'), may hold values from -0.3125 to 0.3125
- w_in_slot: int32 [2, 4, 4, 64], P('section', 'row', 'col'), may hold values from 0 to 575, as said below
- w_in_count: int32 [2, 4, 4], P('section', 'row', 'col'), may hold values from 16 to 64, as said below
- w_out: bfloat16 [2, 4, 4, 64, 128, 128], P('section', 'row', 'col'), may hold values from -0.15625 to 0.15625
- w_out_slot: int32 [2, 4, 4, 64], P('section', 'row', 'col'), may hold values from 0 to 575, as said below
- w_out_count: int32 [2, 4, 4], P('section', 'row', 'col'), may hold values from 16 to 64, as said below
Outputs:
- phase_outputs: bfloat16 [2, 2, 512, 6144], P('section', None, 'row', 'col')
Inputs may be any that keep to these rules, and one draw needn't show every extreme that they name: `w_in_slot`: positions p = d * 48 + f of a block in its cell's 12 x 48 grid of blocks; distinct within a cell; slots at or beyond the cell's count are ignored. `w_in_count`: used slots are the leading ones; in every phase each grid row has a cell with exactly 64. `w_out_slot`: positions p = d * 48 + f of a block in its cell's 12 x 48 grid of blocks; distinct within a cell; slots at or beyond the cell's count are ignored. `w_out_count`: used slots are the leading ones; in every phase each grid row has a cell with exactly 64.
All inputs are finite; a program needn't handle non-finite values.
Results may differ from a plain program's by a relative error of at most 0.012.
Values may be sent and summed in bfloat16 or wider, within the bound.
A program may use at most 128 MiB of HBM per device.

v0:
```python
import jax
import jax.numpy as jnp
from jax import lax
from jax.sharding import PartitionSpec as P

FF = 24576


EPSILON = 1e-05


def shifted(block, axis, distance):
    devices = range(lax.axis_size(axis))
    route = [(i - distance, i) for i in devices if i - distance in devices]
    return lax.ppermute(block, axis, route)


def unpack(blocks, slot_ids, counts, d_blocks, hidden_blocks):
    sources = blocks.shape[1]
    slot_count = blocks.shape[3]
    width_block = blocks.shape[5]
    stacked = blocks.reshape(sources * slot_count, width_block, width_block)
    slot_flat = slot_ids.reshape(sources * slot_count)
    usable = (
        jnp.arange(slot_count, dtype=jnp.int32)[None, :] < counts.reshape(sources, 1)
    ).reshape(sources * slot_count)
    stacked = jnp.where(usable[:, None, None], stacked, jnp.zeros((), stacked.dtype))
    anchor = jnp.repeat(jnp.arange(sources, dtype=jnp.int32), slot_count)
    model_block = anchor * d_blocks + slot_flat // hidden_blocks
    hidden_block = slot_flat % hidden_blocks
    return (stacked, model_block, hidden_block)


def block_sum(dense_rows, picked, stacked, target, span_blocks):
    chosen = jnp.take(dense_rows, picked, axis=1)
    products = jnp.einsum("mek,ekf->mef", chosen, stacked, preferred_element_type=jnp.float32)
    totals = jnp.zeros((dense_rows.shape[0], span_blocks, stacked.shape[2]), jnp.float32)
    return totals.at[:, target].add(products)


def shards(inputs, norm_gain, w_in, w_in_slot, w_in_count, w_out, w_out_slot, w_out_count):
    phase_idx = lax.axis_index("section")
    col_idx = lax.axis_index("col")
    col_total = lax.axis_size("col")
    row_total = lax.axis_size("row")
    phase_total = lax.axis_size("section")
    micro_count = inputs.shape[0]
    token_rows = inputs.shape[1]
    model_width = inputs.shape[2]
    shard_width = model_width // col_total
    block_width = w_in.shape[-1]
    all_blocks = model_width // block_width
    d_blocks = all_blocks // row_total
    hidden_blocks = FF // block_width // col_total
    gathered = (
        lax.all_gather(w_in, "row", axis=1, tiled=True),
        lax.all_gather(w_in_slot, "row", axis=1, tiled=True),
        lax.all_gather(w_in_count, "row", axis=1, tiled=True),
        lax.all_gather(w_out, "row", axis=1, tiled=True),
        lax.all_gather(w_out_slot, "row", axis=1, tiled=True),
        lax.all_gather(w_out_count, "row", axis=1, tiled=True),
    )
    in_stack, in_model, in_hidden = unpack(
        gathered[0], gathered[1], gathered[2], d_blocks, hidden_blocks
    )
    out_stack, out_model, out_hidden = unpack(
        gathered[3], gathered[4], gathered[5], d_blocks, hidden_blocks
    )
    gain_row = norm_gain[0]
    tick_count = phase_total + micro_count - 1
    stored = jnp.zeros((micro_count, token_rows, shard_width), jnp.bfloat16)
    arriving = jnp.zeros((token_rows, shard_width), jnp.bfloat16)
    for tick_idx in range(tick_count):
        if tick_idx < micro_count:
            own_slice = lax.dynamic_slice_in_dim(
                inputs[tick_idx], col_idx * shard_width, shard_width, 1
            )
            current = jnp.where(phase_idx == 0, own_slice, arriving)
        else:
            current = arriving
        full_rows = lax.all_gather(current, "col", axis=1, tiled=True)
        as_float = full_rows.astype(jnp.float32)
        scaled = (
            as_float
            * lax.rsqrt(jnp.mean(as_float * as_float, axis=1, keepdims=True) + EPSILON)
            * gain_row[None, :]
        )
        normed = scaled.astype(jnp.bfloat16)
        before = block_sum(
            normed.reshape(token_rows, all_blocks, block_width),
            in_model,
            in_stack,
            in_hidden,
            hidden_blocks,
        )
        hidden = jax.nn.gelu(before.reshape(token_rows, hidden_blocks * block_width)).astype(
            jnp.bfloat16
        )
        summed = block_sum(
            hidden.reshape(token_rows, hidden_blocks, block_width),
            out_hidden,
            out_stack,
            out_model,
            all_blocks,
        )
        summed = lax.psum_scatter(
            lax.optimization_barrier(summed.reshape(token_rows, model_width).astype(jnp.bfloat16))
            .astype(jnp.float32)
            .astype(jnp.bfloat16),
            "col",
            scatter_dimension=1,
            tiled=True,
        ).astype(jnp.float32)
        result = (current.astype(jnp.float32) + summed).astype(jnp.bfloat16)
        wanted = jnp.arange(micro_count, dtype=jnp.int32) == tick_idx - phase_idx
        stored = jnp.where(wanted[:, None, None], result[None], stored)
        if tick_idx + 1 < tick_count:
            arriving = shifted(result, "section", 1)
    return stored[None]


def solution(mesh):
    placed = (
        P(None, "row", None),
        P("section", None),
        P("section", "row", "col", None, None, None),
        P("section", "row", "col", None),
        P("section", "row", "col"),
        P("section", "row", "col", None, None, None),
        P("section", "row", "col", None),
        P("section", "row", "col"),
    )
    return jax.shard_map(
        shards,
        mesh=mesh,
        in_specs=placed,
        out_specs=P("section", None, "row", "col"),
        check_vma=False,
    )
```

profile of v0, /device:TPU:1, one launch (start us, length us, event | category | flops | bytes accessed | tf_op | source)
XLA Modules:
  0.0 827.4 jit_solution(11766204215724026871)
XLA Ops:
  49.4 8.9 %gather_fusion = bf16[256,128,128]{2,1,0:T(8,128)(2,1)} fusion(bf16[128,48,128]{2,0,1:T(8,128)(2,1)S(1)} %copy.47, s32[1024]{0:T(1024)S(1)} %pad_clamp_fusion.1), kind=kCustom, calls=%fused_computation.clone | custom fusion | bytes 16778240 | tf_op jit(solution)/shard_map/jit(_take)/gather | solution.py:35
  58.4 137.2 %all-gather.9.cloned.1.call-done = bf16[1,4,1,64,128,128]{5,4,3,2,0,1:T(8,128)(2,1)} async-done(((bf16[1,1,1,64,128,128]{5,4,3,2,0,1:T(8,128)(2,1)}), bf16[1,4,1,64,128,128]{5,4,3,2,0,1:T(8,128)(2,1)}) %all-gather.9.cloned.1.call-update) | async-done | bytes 8388624 | tf_op jit(solution)/shard_map/all_gather | solution.py:56
  203.0 15.4 %fusion.10 = f32[256,128,128]{2,1,0:T(8,128)} fusion(bf16[256,128,128]{2,1,0:T(8,128)(2,1)} %bitcast_select_fusion.1, bf16[256,128,128]{2,1,0:T(8,128)(2,1)} %gather_fusion, pred[256]{0:T(512)(128)(4,1)S(1)} %copy-done.10), kind=kOutput, calls=%fused_computation.24 | convolution fusion | flops 1077936128 | bytes 33554688 | tf_op jit(solution)/shard_map/mek,ekf->mef/dot_general | solution.py:36
  218.8 33.3 %scatter_fusion = f32[128,48,128]{2,0,1:T(8,128)S(1)} fusion(f32[128,48,128]{2,0,1:T(8,128)S(1)} %broadcast.277.clone.1, s32[256]{0:T(256)S(1)} %bitcast.66, f32[256,128,128]{2,1,0:T(8,128)} %fusion.10), kind=kCustom, calls=%fused_computation.6 | custom fusion | flops 4194304 | bytes 50332672 | tf_op jit(solution)/shard_map/scatter-add | solution.py:38
  254.4 10.4 %gather_fusion.1 = bf16[256,128,128]{2,1,0:T(8,128)(2,1)} fusion(bf16[128,48,128]{2,0,1:T(8,128)(2,1)} %fusion.46, s32[1024]{0:T(1024)S(1)} %pad_clamp_fusion), kind=kCustom, calls=%fused_computation.1.clone | custom fusion | bytes 16778240 | tf_op jit(solution)/shard_map/jit(_take)/gather | solution.py:35
  264.8 80.3 %all-gather.7.cloned.1.call-done = bf16[1,4,1,64,128,128]{5,4,3,2,0,1:T(8,128)(2,1)} async-done(((bf16[1,1,1,64,128,128]{5,4,3,2,0,1:T(8,128)(2,1)}), bf16[1,4,1,64,128,128]{5,4,3,2,0,1:T(8,128)(2,1)}) %all-gather.7.cloned.1.call-update) | async-done | bytes 8388624 | tf_op jit(solution)/shard_map/all_gather | solution.py:59
  352.3 13.9 %fusion.8 = f32[256,128,128]{2,1,0:T(8,128)} fusion(bf16[256,128,128]{2,1,0:T(8,128)(2,1)} %bitcast_select_fusion, bf16[256,128,128]{2,1,0:T(8,128)(2,1)} %gather_fusion.1, pred[256]{0:T(512)(128)(4,1)S(1)} %copy-done.7), kind=kOutput, calls=%fused_computation.21 | convolution fusion | flops 1077936128 | bytes 33554688 | tf_op jit(solution)/shard_map/mek,ekf->mef/dot_general | solution.py:36
  366.6 33.2 %scatter_fusion.1 = f32[128,48,128]{2,0,1:T(8,128)S(1)} fusion(f32[128,48,128]{2,0,1:T(8,128)S(1)} %broadcast.277.clone, s32[256]{0:T(256)S(1)} %bitcast.69, f32[256,128,128]{2,1,0:T(8,128)} %fusion.8), kind=kCustom, calls=%fused_computation.7 | custom fusion | flops 4194304 | bytes 50332672 | tf_op jit(solution)/shard_map/scatter-add | solution.py:38
  403.8 29.1 %reduce-scatter.4.cloned.1.call-done = bf16[128,1536]{0,1:T(8,128)(2,1)} async-done(((bf16[128,6144]{0,1:T(8,128)(2,1)}), bf16[128,1536]{0,1:T(8,128)(2,1)}) %reduce-scatter.4.cloned.1.call-update) | async-done | bytes 393232 | tf_op jit(solution)/shard_map/reduce_scatter | solution.py:106
  438.5 30.6 %all-gather.11.cloned.1.call-done = bf16[128,6144]{0,1:T(8,128)(2,1)} async-done(((bf16[128,1536]{0,1:T(8,128)(2,1)}), bf16[128,6144]{0,1:T(8,128)(2,1)}) %all-gather.11.cloned.1.call-update) | async-done | bytes 1572880 | tf_op jit(solution)/shard_map/all_gather | solution.py:81
  483.0 13.9 %fusion.6 = f32[256,128,128]{2,1,0:T(8,128)} fusion(bf16[256,128,128]{2,1,0:T(8,128)(2,1)} %bitcast_select_fusion.1, bf16[256,128,128]{2,1,0:T(8,128)(2,1)} %gather_fusion.2, pred[256]{0:T(512)(128)(4,1)S(1)} %copy-done.11), kind=kOutput, calls=%fused_computation.18 | convolution fusion | flops 1077936128 | bytes 33554688 | tf_op jit(solution)/shard_map/mek,ekf->mef/dot_general | solution.py:36
  497.2 33.2 %scatter_fusion.2 = f32[128,48,128]{2,0,1:T(8,128)S(1)} fusion(f32[128,48,128]{2,0,1:T(8,128)S(1)} %broadcast.277.clone.3, s32[256]{0:T(256)S(1)} %bitcast.67, f32[256,128,128]{2,1,0:T(8,128)} %fusion.6), kind=kCustom, calls=%fused_computation.8 | custom fusion | flops 4194304 | bytes 50332672 | tf_op jit(solution)/shard_map/scatter-add | solution.py:38
  532.6 10.1 %gather_fusion.3 = bf16[256,128,128]{2,1,0:T(8,128)(2,1)} fusion(bf16[128,48,128]{2,0,1:T(8,128)(2,1)} %fusion.54, s32[1024]{0:T(1024)S(1)} %pad_clamp_fusion), kind=kCustom, calls=%fused_computation.3.clone | custom fusion | bytes 16778240 | tf_op jit(solution)/shard_map/jit(_take)/gather | solution.py:35
  542.8 13.9 %fusion.4 = f32[256,128,128]{2,1,0:T(8,128)} fusion(bf16[256,128,128]{2,1,0:T(8,128)(2,1)} %bitcast_select_fusion, bf16[256,128,128]{2,1,0:T(8,128)(2,1)} %gather_fusion.3, pred[256]{0:T(512)(128)(4,1)S(1)} %copy-done.8), kind=kOutput, calls=%fused_computation.16 | convolution fusion | flops 1077936128 | bytes 33554688 | tf_op jit(solution)/shard_map/mek,ekf->mef/dot_general | solution.py:36
  557.1 33.2 %scatter_fusion.3 = f32[128,48,128]{2,0,1:T(8,128)S(1)} fusion(f32[128,48,128]{2,0,1:T(8,128)S(1)} %broadcast.277.clone.2, s32[256]{0:T(256)S(1)} %bitcast.70, f32[256,128,128]{2,1,0:T(8,128)} %fusion.4), kind=kCustom, calls=%fused_computation.9 | custom fusion | flops 4194304 | bytes 50332672 | tf_op jit(solution)/shard_map/scatter-add | solution.py:38
  594.4 31.0 %reduce-scatter.6.cloned.1.call-done = bf16[128,1536]{0,1:T(8,128)(2,1)} async-done(((bf16[128,6144]{0,1:T(8,128)(2,1)}), bf16[128,1536]{0,1:T(8,128)(2,1)}) %reduce-scatter.6.cloned.1.call-update) | async-done | bytes 393232 | tf_op jit(solution)/shard_map/reduce_scatter | solution.py:106
  631.0 30.6 %all-gather.13.cloned.1.call-done = bf16[128,6144]{0,1:T(8,128)(2,1)} async-done(((bf16[128,1536]{0,1:T(8,128)(2,1)}), bf16[128,6144]{0,1:T(8,128)(2,1)}) %all-gather.13.cloned.1.call-update) | async-done | bytes 1572880 | tf_op jit(solution)/shard_map/all_gather | solution.py:81
  666.8 8.6 %gather_fusion.4 = bf16[256,128,128]{2,1,0:T(8,128)(2,1)} fusion(bf16[128,48,128]{2,0,1:T(8,128)(2,1)S(1)} %copy.53, s32[1024]{0:T(1024)S(1)} %pad_clamp_fusion.1), kind=kCustom, calls=%fused_computation.4.clone | custom fusion | bytes 16778240 | tf_op jit(solution)/shard_map/jit(_take)/gather | solution.py:35
  675.4 13.9 %fusion.2 = f32[256,128,128]{2,1,0:T(8,128)} fusion(bf16[256,128,128]{2,1,0:T(8,128)(2,1)} %bitcast_select_fusion.1, bf16[256,128,128]{2,1,0:T(8,128)(2,1)} %gather_fusion.4, pred[256]{0:T(512)(128)(4,1)S(1)} %copy-done.12), kind=kOutput, calls=%fused_computation.14 | convolution fusion | flops 1077936128 | bytes 33554688 | tf_op jit(solution)/shard_map/mek,ekf->mef/dot_general | solution.py:36
  689.7 33.2 %scatter_fusion.4 = f32[128,48,128]{2,0,1:T(8,128)S(1)} fusion(f32[128,48,128]{2,0,1:T(8,128)S(1)} %broadcast.277.clone.4, s32[256]{0:T(256)S(1)} %bitcast.68, f32[256,128,128]{2,1,0:T(8,128)} %fusion.2), kind=kCustom, calls=%fused_computation.10 | custom fusion | flops 4194304 | bytes 50332672 | tf_op jit(solution)/shard_map/scatter-add | solution.py:38
  725.1 10.2 %gather_fusion.5 = bf16[256,128,128]{2,1,0:T(8,128)(2,1)} fusion(bf16[128,48,128]{2,0,1:T(8,128)(2,1)} %fusion.62, s32[1024]{0:T(1024)S(1)} %pad_clamp_fusion), kind=kCustom, calls=%fused_computation.5.clone | custom fusion | bytes 16778240 | tf_op jit(solution)/shard_map/jit(_take)/gather | solution.py:35
  735.3 13.9 %fusion = f32[256,128,128]{2,1,0:T(8,128)} fusion(bf16[256,128,128]{2,1,0:T(8,128)(2,1)} %bitcast_select_fusion, bf16[256,128,128]{2,1,0:T(8,128)(2,1)} %gather_fusion.5, pred[256]{0:T(512)(128)(4,1)S(1)} %copy-done.9), kind=kOutput, calls=%fused_computation.12 | convolution fusion | flops 1077936128 | bytes 33554688 | tf_op jit(solution)/shard_map/mek,ekf->mef/dot_general | solution.py:36
  749.6 33.2 %scatter_fusion.5 = f32[128,48,128]{2,0,1:T(8,128)S(1)} fusion(f32[128,48,128]{2,0,1:T(8,128)S(1)} %broadcast.277, s32[256]{0:T(256)S(1)} %bitcast.71, f32[256,128,128]{2,1,0:T(8,128)} %fusion), kind=kCustom, calls=%fused_computation.11 | custom fusion | flops 4194304 | bytes 50332672 | tf_op jit(solution)/shard_map/scatter-add | solution.py:38
  787.3 30.7 %reduce-scatter.8.cloned.1.call-done = bf16[128,1536]{0,1:T(8,128)(2,1)} async-done(((bf16[128,6144]{0,1:T(8,128)(2,1)}), bf16[128,1536]{0,1:T(8,128)(2,1)}) %reduce-scatter.8.cloned.1.call-update) | async-done | bytes 393232 | tf_op jit(solution)/shard_map/reduce_scatter | solution.py:106
  (133 shorter events, 110.1 us)
Async XLA Ops:
  6.5 37.6 %all-gather.15.cloned.1.call-start = ((), (), s32[]{:S(2)}) async-start(), calls=%async_computation.10 | async-start | bytes 1966080 | tf_op jit(solution)/shard_map/all_gather | solution.py:81
  9.9 13.3 %copy-start.15 = (s32[1,1,1,64]{3,2,1,0:T(1,128)S(1)}, s32[1,1,1,64]{3,2,1,0:T(1,128)}, u32[]{:S(2)}) copy-start(s32[1,1,1,64]{3,2,1,0:T(1,128)} %param.16) | copy-start | bytes 772
  9.9 20.4 %copy-start.16 = (s32[1,1,1,64]{3,2,1,0:T(1,128)S(1)}, s32[1,1,1,64]{3,2,1,0:T(1,128)}, u32[]{:S(2)}) copy-start(s32[1,1,1,64]{3,2,1,0:T(1,128)} %param.13) | copy-start | bytes 772
  10.9 35.5 %copy-start.5 = (f32[1,6144]{1,0:T(1,128)S(1)}, f32[1,6144]{1,0:T(1,128)}, u32[]{:S(2)}) copy-start(f32[1,6144]{1,0:T(1,128)} %param.11) | copy-start | bytes 73732
  10.9 184.7 %all-gather.9.cloned.1.call-start = ((), (), s32[]{:S(2)}) async-start(), calls=%async_computation.4 | async-start | bytes 10485760 | tf_op jit(solution)/shard_map/all_gather | solution.py:56
  11.7 333.4 %all-gather.7.cloned.1.call-start = ((), (), s32[]{:S(2)}) async-start(), calls=%async_computation.3 | async-start | bytes 10485760 | tf_op jit(solution)/shard_map/all_gather | solution.py:59
  12.4 420.5 %reduce-scatter.4.cloned.1.call-start = ((), (), s32[]{:S(2)}) async-start(), calls=%async_computation.5 | async-start | bytes 1966080 | tf_op jit(solution)/shard_map/reduce_scatter | solution.py:106
  49.4 146.2 %copy-start.14 = (pred[256]{0:T(512)(128)(4,1)S(1)}, pred[256]{0:T(512)(128)(4,1)}, u32[]{:S(2)}) copy-start(pred[256]{0:T(512)(128)(4,1)} %lt.101) | copy-start | bytes 772
  58.4 144.6 %copy-start.10 = (pred[256]{0:T(512)(128)(4,1)S(1)}, pred[256]{0:T(512)(128)(4,1)}, u32[]{:S(2)}) copy-start(pred[256]{0:T(512)(128)(4,1)} %get-tuple-element.14) | copy-start | bytes 772
  254.4 90.7 %copy-start.13 = (pred[256]{0:T(512)(128)(4,1)S(1)}, pred[256]{0:T(512)(128)(4,1)}, u32[]{:S(2)}) copy-start(pred[256]{0:T(512)(128)(4,1)} %lt.94) | copy-start | bytes 772
  264.8 87.5 %copy-start.7 = (pred[256]{0:T(512)(128)(4,1)S(1)}, pred[256]{0:T(512)(128)(4,1)}, u32[]{:S(2)}) copy-start(pred[256]{0:T(512)(128)(4,1)} %get-tuple-element.12) | copy-start | bytes 772
  403.8 65.3 %all-gather.11.cloned.1.call-start = ((), (), s32[]{:S(2)}) async-start(), calls=%async_computation.6 | async-start | bytes 1966080 | tf_op jit(solution)/shard_map/all_gather | solution.py:81
  434.0 39.5 %copy-start.1 = (bf16[128,1536]{0,1:T(8,128)(2,1)}, bf16[128,1536]{0,1:T(8,128)(2,1)S(1)}, u32[]{:S(2)}) copy-start(bf16[128,1536]{0,1:T(8,128)(2,1)S(1)} %fusion.63) | copy-start | bytes 1179652
  434.0 3.6 collective-permute-start
  438.5 186.9 %reduce-scatter.6.cloned.1.call-start = ((), (), s32[]{:S(2)}) async-start(), calls=%async_computation.7 | async-start | bytes 1966080 | tf_op jit(solution)/shard_map/reduce_scatter | solution.py:106
  474.4 8.6 %copy-start.11 = (pred[256]{0:T(512)(128)(4,1)S(1)}, pred[256]{0:T(512)(128)(4,1)}, u32[]{:S(2)}) copy-start(pred[256]{0:T(512)(128)(4,1)} %get-tuple-element.14) | copy-start | bytes 772
  532.6 10.2 %copy-start.8 = (pred[256]{0:T(512)(128)(4,1)S(1)}, pred[256]{0:T(512)(128)(4,1)}, u32[]{:S(2)}) copy-start(pred[256]{0:T(512)(128)(4,1)} %get-tuple-element.12) | copy-start | bytes 772
  591.6 33.8 %copy-start = (bf16[128,1536]{0,1:T(8,128)(2,1)S(1)}, bf16[128,1536]{0,1:T(8,128)(2,1)}, u32[]{:S(2)}) copy-start(bf16[128,1536]{0,1:T(8,128)(2,1)} %bitcast_select_fusion.2) | copy-start | bytes 1179652
  594.3 69.5 %copy-start.6 = (f32[1,6144]{1,0:T(1,128)S(1)}, f32[1,6144]{1,0:T(1,128)}, u32[]{:S(2)}) copy-start(f32[1,6144]{1,0:T(1,128)} %param.11) | copy-start | bytes 73732
  594.3 67.2 %all-gather.13.cloned.1.call-start = ((), (), s32[]{:S(2)}) async-start(), calls=%async_computation.8 | async-start | bytes 1966080 | tf_op jit(solution)/shard_map/all_gather | solution.py:81
  626.5 3.6 collective-permute-start.1
  630.9 187.0 %reduce-scatter.8.cloned.1.call-start = ((), (), s32[]{:S(2)}) async-start(), calls=%async_computation.9 | async-start | bytes 1966080 | tf_op jit(solution)/shard_map/reduce_scatter | solution.py:106
  725.1 10.2 %copy-start.9 = (pred[256]{0:T(512)(128)(4,1)S(1)}, pred[256]{0:T(512)(128)(4,1)}, u32[]{:S(2)}) copy-start(pred[256]{0:T(512)(128)(4,1)} %get-tuple-element.12) | copy-start | bytes 772
  784.1 33.8 %copy-start.4 = (bf16[128,1536]{0,1:T(8,128)(2,1)S(1)}, bf16[128,1536]{0,1:T(8,128)(2,1)}, u32[]{:S(2)}) copy-start(bf16[128,1536]{0,1:T(8,128)(2,1)} %copy-done.3) | copy-start | bytes 1179652
  (4 other events, 16.0 us)
Sparse Core Ops, SparseCore 0:
  11.1 33.0 all-gather.14
  45.7 149.8 all-gather.8
  197.2 147.8 all-gather.6
  403.9 28.9 reduce-scatter.3
  438.6 30.4 all-gather.10
  594.4 30.9 reduce-scatter.5
  631.1 30.4 all-gather.12
  787.0 30.9 reduce-scatter.7
where the time goes:
time: 842 us; the launch traced here: 827 us
  waiting for transfers between devices  378 us (45%)
  other arithmetic  245 us (29%)
  matrix products  84.9 us (10%)
  local copies, waits for them, and re-layouts  79.8 us (9%)
  blocking collectives  21.1 us (3%)
  between operations  15.5 us (2%)
    scatter-add x6, other arithmetic, block_sum(): return totals.at[:, target].add(products)  199 us
    all_gather x1, waiting for transfers between devices, shards(): lax.all_gather(w_in, 'row', axis=1, tiled=True)  137 us
    reduce_scatter x3, waiting for transfers between devices, shards(): lax.psum_scatter(lax.optimization_barrier(summed.reshape(token_rows, mode...  90.8 us
    dot_general x6, matrix products, block_sum(): jnp.einsum('mek,ekf->mef', chosen, stacked, preferred_element_type=jnp.fl...  84.9 us
    all_gather x1, waiting for transfers between devices, shards(): lax.all_gather(w_out, 'row', axis=1, tiled=True)  80.3 us
    all_gather x3, waiting for transfers between devices, shards(): full_rows = lax.all_gather(current, 'col', axis=1, tiled=True)  65 us
    gather x6, local copies, waits for them, and re-layouts, block_sum(): chosen = jnp.take(dense_rows, picked, axis=1)  56.9 us
  transfers between devices with their start and end apart: 10, of which 10 were waited for; matrix products, arithmetic and copies ran while one was open for 11% of the time, Pallas kernels for 0%

commit v1 on v0

v1 whole, which is shorter than its diff:
```python
import functools

import jax
import jax.numpy as jnp
from jax import lax
from jax.experimental import pallas as pl
from jax.experimental.pallas import tpu as pltpu
from jax.sharding import PartitionSpec as P

FF = 24576


EPSILON = 1e-05
UNROLL = 4


def add_blocks(acc, source, weights, slots, counts, offset, d_blocks, f_blocks, into_hidden):
    cells, slot_count = weights.shape[0], weights.shape[1]
    step = UNROLL if slot_count % UNROLL == 0 else 1

    def cell_body(cell, carry):
        count = counts[offset + cell]

        def group(g, inner):
            products = []
            for j in range(step):
                n = g * step + j
                usable = n < count
                p = jnp.where(usable, slots[(offset + cell) * slot_count + n], 0)
                d = cell * d_blocks + lax.div(p, f_blocks)
                f = lax.rem(p, f_blocks)
                src, dst = (d, f) if into_hidden else (f, d)
                w = weights[cell, n]
                w = jnp.where(usable, w, jnp.zeros_like(w))
                products.append(
                    (dst, jnp.dot(source[src], w, preferred_element_type=jnp.float32))
                )
            for dst, value in products:
                acc[dst] += value
            return inner

        lax.fori_loop(0, lax.div(count + step - 1, step), group, 0)
        return carry

    lax.fori_loop(0, cells, cell_body, 0)


def ffn_kernel(d_blocks, f_blocks, slots, counts, x, gain, w_in, w_out, out, normed, hidden, acc):
    cells = w_in.shape[0]
    all_d = cells * d_blocks
    tokens = x.shape[0]
    blk = w_in.shape[-1]
    total = jnp.zeros((tokens, 1), jnp.float32)
    for d in range(all_d):
        part = x[:, d * blk : (d + 1) * blk].astype(jnp.float32)
        total = total + jnp.sum(part * part, axis=1, keepdims=True)
    scale = lax.rsqrt(total / (all_d * blk) + EPSILON)
    for d in range(all_d):
        cols = slice(d * blk, (d + 1) * blk)
        normed[d] = (x[:, cols].astype(jnp.float32) * scale * gain[:, cols]).astype(jnp.bfloat16)

    def clear(i, carry):
        acc[i] = jnp.zeros_like(acc[i])
        return carry

    lax.fori_loop(0, f_blocks, clear, 0)
    add_blocks(acc, normed, w_in, slots, counts, 0, d_blocks, f_blocks, True)

    def activate(i, carry):
        hidden[i] = jax.nn.gelu(acc[i]).astype(jnp.bfloat16)
        return carry

    lax.fori_loop(0, f_blocks, activate, 0)
    lax.fori_loop(0, all_d, clear, 0)
    add_blocks(acc, hidden, w_out, slots, counts, cells, d_blocks, f_blocks, False)
    for d in range(all_d):
        out[:, d * blk : (d + 1) * blk] = acc[d].astype(jnp.bfloat16)


def ffn(x, gain, w_in, w_out, slots, counts, d_blocks, f_blocks):
    tokens, width = x.shape
    blk = w_in.shape[-1]
    vmem = pl.BlockSpec(memory_space=pltpu.VMEM)
    smem = pl.BlockSpec(memory_space=pltpu.SMEM)
    all_d = width // blk
    return pl.pallas_call(
        functools.partial(ffn_kernel, d_blocks, f_blocks),
        out_shape=jax.ShapeDtypeStruct((tokens, width), jnp.bfloat16),
        in_specs=[smem, smem, vmem, vmem, vmem, vmem],
        out_specs=vmem,
        scratch_shapes=[
            pltpu.VMEM((all_d, tokens, blk), jnp.bfloat16),
            pltpu.VMEM((f_blocks, tokens, blk), jnp.bfloat16),
            pltpu.VMEM((max(all_d, f_blocks), tokens, blk), jnp.float32),
        ],
        compiler_params=pltpu.CompilerParams(vmem_limit_bytes=52 * 2**20),
    )(slots, counts, x, gain, w_in, w_out)


def shards(inputs, norm_gain, w_in, w_in_slot, w_in_count, w_out, w_out_slot, w_out_count):
    phase_idx = lax.axis_index("section")
    col_idx = lax.axis_index("col")
    col_total = lax.axis_size("col")
    row_total = lax.axis_size("row")
    micro_count, token_rows, model_width = inputs.shape
    shard_width = model_width // col_total
    blk = w_in.shape[-1]
    d_blocks = model_width // blk // row_total
    f_blocks = FF // blk // col_total
    slot_count = w_in.shape[3]
    meta = jnp.concatenate(
        [w_in_slot.reshape(-1), w_out_slot.reshape(-1), w_in_count.reshape(-1), w_out_count.reshape(-1)]
    )
    meta = lax.all_gather(meta, "row", axis=0)
    slots = jnp.concatenate(
        [meta[:, :slot_count].reshape(-1), meta[:, slot_count : 2 * slot_count].reshape(-1)]
    )
    counts = jnp.concatenate([meta[:, 2 * slot_count], meta[:, 2 * slot_count + 1]])
    all_in = lax.all_gather(w_in[0, 0, 0], "row", axis=0)
    all_out = lax.all_gather(w_out[0, 0, 0], "row", axis=0)
    tokens = micro_count * token_rows

    current_full = inputs.reshape(tokens, model_width)
    current = lax.dynamic_slice_in_dim(current_full, col_idx * shard_width, shard_width, 1)
    results = []
    phases = lax.axis_size("section")
    for phase in range(phases):
        part = ffn(current_full, norm_gain, all_in, all_out, slots, counts, d_blocks, f_blocks)
        branch = lax.psum_scatter(part, "col", scatter_dimension=1, tiled=True)
        result = (current.astype(jnp.float32) + branch.astype(jnp.float32)).astype(jnp.bfloat16)
        results.append(result)
        if phase + 1 < phases:
            current = lax.ppermute(result, "section", [(i, i + 1) for i in range(phases - 1)])
            current_full = lax.all_gather(current, "col", axis=1, tiled=True)
    out = results[0]
    for phase in range(1, phases):
        out = jnp.where(phase_idx == phase, results[phase], out)
    return out.reshape(1, micro_count, token_rows, shard_width)


def solution(mesh):
    placed = (
        P(None, "row", None),
        P("section", None),
        P("section", "row", "col", None, None, None),
        P("section", "row", "col", None),
        P("section", "row", "col"),
        P("section", "row", "col", None, None, None),
        P("section", "row", "col", None),
        P("section", "row", "col"),
    )
    return jax.shard_map(
        shards,
        mesh=mesh,
        in_specs=placed,
        out_specs=P("section", None, "row", "col"),
        check_vma=False,
    )
```

time: 842 us -> 532 us (0.63); the launches traced: 827 us -> 538 us
  other arithmetic: 245 us -> 4.11 us
  matrix products: 84.9 us -> 0 us
  waiting for transfers between devices: 378 us -> 456 us
  local copies, waits for them, and re-layouts: 79.8 us -> 2.01 us
  Pallas kernels: 0 us -> 51.1 us
  blocking collectives: 21.1 us -> 7.25 us
    scatter-add x6 -> x0, other arithmetic: 199 us -> none  [block_sum(): return totals.at[:, target].add(products)]
    dot_general x6 -> x0, matrix products: 84.9 us -> none  [block_sum(): jnp.einsum('mek,ekf->mef', chosen, stacked, preferred_element_type=jnp.fl...]
    gather x6 -> x0, local copies, waits for them, and re-layouts: 56.9 us -> none  [block_sum(): chosen = jnp.take(dense_rows, picked, axis=1)]
    all_gather x5 -> x3, waiting for transfers between devices: 282 us -> 335 us  [the longest x1 149 us: shards(): all_out = lax.all_gather(w_out[0, 0, 0], 'row', axis=0)]
    pallas_call x0 -> x2, Pallas kernels: none -> 51.1 us  [ffn(): pl.pallas_call(functools.partial(ffn_kernel, d_blocks, f_blocks), out_sha...]
    reduce_scatter x3 -> x2, waiting for transfers between devices: 90.8 us -> 117 us  [shards(): branch = lax.psum_scatter(part, 'col', scatter_dimension=1, tiled=True)]
    convert_element_type x12 -> x1, other arithmetic: 20.5 us -> 1.56 us  [shards(): (current.astype(jnp.float32) + branch.astype(jnp.float32)).astype(jnp.bfl...]
    select_n x7 -> x1, other arithmetic: 17.3 us -> 2.29 us  [shards(): out = jnp.where(phase_idx == phase, results[phase], out)]
  transfers between devices with their start and end apart: 10 -> 6, of which waited for: 10 -> 6; matrix products, arithmetic and copies ran while one was open for 11% -> 0% of each run, Pallas kernels for 0% -> 0%
where the time goes in v1:
time: 532 us; the launch traced here: 538 us
  waiting for transfers between devices  456 us (86%)
  Pallas kernels  51.1 us (10%)
  between operations  15.2 us (3%)
  blocking collectives  7.25 us (1%)
    all_gather x1, waiting for transfers between devices, shards(): all_out = lax.all_gather(w_out[0, 0, 0], 'row', axis=0)  149 us
    all_gather x1, waiting for transfers between devices, shards(): all_in = lax.all_gather(w_in[0, 0, 0], 'row', axis=0)  142 us
    reduce_scatter x2, waiting for transfers between devices, shards(): branch = lax.psum_scatter(part, 'col', scatter_dimension=1, tiled=True)  117 us
    pallas_call x2, Pallas kernels, ffn(): pl.pallas_call(functools.partial(ffn_kernel, d_blocks, f_blocks), out_sha...  51.1 us
    all_gather x1, waiting for transfers between devices, shards(): current_full = lax.all_gather(current, 'col', axis=1, tiled=True)  43.6 us
  transfers between devices with their start and end apart: 6, of which 6 were waited for; matrix products, arithmetic and copies ran while one was open for 0% of the time, Pallas kernels for 0%

profile of v1, /device:TPU:1, one launch (start us, length us, event | category | flops | bytes accessed | tf_op | source)
XLA Modules:
  0.0 537.6 jit_solution(8809250496114567178)
XLA Ops:
  6.6 0.7 all-gather.9.cloned.1.call-update
  7.3 0.7 all-gather.11.cloned.1.call-update
  9.4 0.6 dynamic-slice
  10.7 0.2 add_dynamic-update-slice_fusion
  10.9 7.3 %all-reduce = s32[520]{0:T(1024)S(1)} all-reduce(s32[520]{0:T(1024)S(1)} %add_dynamic-update-slice_fusion), channel_id=2, replica_groups=mesh['section'=2,'row'=4,'col'=4] {'row'}, use_global_device_ids=true, to_apply=%add | all-reduce | flops 520 | bytes 4160
  18.1 0.1 reshape.32
  18.2 0.1 fusion.1
  18.3 0.1 reshape.30
  18.3 0.1 reshape.29
  18.4 0.2 slice_reduce_fusion.1
  18.6 0.1 pad_add_fusion.counts
  18.7 142.2 %all-gather.9.cloned.1.call-done = bf16[4,1,1,64,128,128]{5,4,3,2,1,0:T(8,128)(2,1)} async-done(((bf16[1,1,1,64,128,128]{5,4,3,2,1,0:T(8,128)(2,1)}), bf16[4,1,1,64,128,128]{5,4,3,2,1,0:T(8,128)(2,1)}) %all-gather.9.cloned.1.call-update) | async-done | bytes 8388624 | tf_op jit(solution)/shard_map/all_gather | solution.py:119
  160.9 149.5 %all-gather.11.cloned.1.call-done = bf16[4,1,1,64,128,128]{5,4,3,2,1,0:T(8,128)(2,1)} async-done(((bf16[1,1,1,64,128,128]{5,4,3,2,1,0:T(8,128)(2,1)}), bf16[4,1,1,64,128,128]{5,4,3,2,1,0:T(8,128)(2,1)}) %all-gather.11.cloned.1.call-update) | async-done | bytes 8388624 | tf_op jit(solution)/shard_map/all_gather | solution.py:120
  310.4 25.6 %shard_map.82 = bf16[256,6144]{1,0:T(8,128)(2,1)} custom-call(s32[512]{0:T(512)S(1)} %constant_dynamic-update-slice_fusion.slots, s32[8]{0:T(128)S(1)} %pad_add_fusion.counts, bf16[256,6144]{1,0:T(8,128)(2,1)} %bitcast.15, f32[1,6144]{1,0:T(1,128)S(1)} %copy-done, bf16[4,64,128,128]{3,2,1,0:T(8,128)(2,1)} %bitcast.11, bf16[4,64,128,128]{3,2,1,0:T(8,128)(2,1)} %bitcast.13), custom_call_target="tpu_custom_call" | custom-call | tf_op jit(solution)/shard_map/pallas_call | solution.py:86
  336.0 57.0 %reduce-scatter.3.cloned.1.call-done = bf16[256,1536]{1,0:T(8,128)(2,1)} async-done(((bf16[256,6144]{1,0:T(8,128)(2,1)}), bf16[256,1536]{1,0:T(8,128)(2,1)}) %reduce-scatter.3.cloned.1.call-update) | async-done | bytes 786448 | tf_op jit(solution)/shard_map/reduce_scatter | solution.py:129
  393.1 1.6 add_convert_fusion.1
  394.6 1.3 collective-permute-start
  395.9 2.9 collective-permute-done
  398.8 0.9 copy-done.1
  399.7 0.0 reduce-scatter.5.cloned.1.call-start
  399.7 43.6 %all-gather.7.cloned.1.call-done.x = bf16[256,6144]{1,0:T(8,128)(2,1)} async-done(((bf16[256,1536]{1,0:T(8,128)(2,1)}), bf16[256,6144]{1,0:T(8,128)(2,1)}) %all-gather.7.cloned.1.call-update) | async-done | bytes 3145744 | tf_op jit(solution)/shard_map/all_gather | solution.py:134
  443.3 25.6 %shard_map.83 = bf16[256,6144]{1,0:T(8,128)(2,1)} custom-call(s32[512]{0:T(512)S(1)} %constant_dynamic-update-slice_fusion.slots, s32[8]{0:T(128)S(1)} %pad_add_fusion.counts, bf16[256,6144]{1,0:T(8,128)(2,1)} %all-gather.7.cloned.1.call-done.x, f32[1,6144]{1,0:T(1,128)S(1)} %copy-done, bf16[4,64,128,128]{3,2,1,0:T(8,128)(2,1)} %bitcast.12, ...), custom_call_target="tpu_custom_call" | custom-call | tf_op jit(solution)/shard_map/pallas_call | solution.py:86
  468.9 59.9 %reduce-scatter.5.cloned.1.call-done = bf16[256,1536]{1,0:T(8,128)(2,1)} async-done(((bf16[256,6144]{1,0:T(8,128)(2,1)}), bf16[256,1536]{1,0:T(8,128)(2,1)}) %reduce-scatter.5.cloned.1.call-update) | async-done | bytes 786448 | tf_op jit(solution)/shard_map/reduce_scatter | solution.py:129
  528.8 2.3 fusion
  (22 shorter events, 0.3 us)
Async XLA Ops:
  6.5 2.9 copy-start.5
  6.5 4.1 copy-start.3
  6.5 4.1 copy-start.4
  6.5 303.8 %copy-start = (f32[1,6144]{1,0:T(1,128)S(1)}, f32[1,6144]{1,0:T(1,128)}, u32[]{:S(2)}) copy-start(f32[1,6144]{1,0:T(1,128)} %gain.3) | copy-start | bytes 73732
  6.5 154.4 %all-gather.9.cloned.1.call-start = ((), (), s32[]{:S(2)}) async-start(), calls=%async_computation.5 | async-start | bytes 10485760 | tf_op jit(solution)/shard_map/all_gather | solution.py:119
  7.3 303.1 %all-gather.11.cloned.1.call-start = ((), (), s32[]{:S(2)}) async-start(), calls=%async_computation.6 | async-start | bytes 10485760 | tf_op jit(solution)/shard_map/all_gather | solution.py:120
  8.0 385.0 %reduce-scatter.3.cloned.1.call-start = ((), (), s32[]{:S(2)}) async-start(), calls=%async_computation.2 | async-start | bytes 3932160 | tf_op jit(solution)/shard_map/reduce_scatter | solution.py:129
  336.0 107.4 %all-gather.7.cloned.1.call-start = ((), (), s32[]{:S(2)}) async-start(), calls=%async_computation.3 | async-start | bytes 3932160 | tf_op jit(solution)/shard_map/all_gather | solution.py:134
  394.6 4.2 collective-permute-start
  398.8 0.9 copy-start.1
  399.7 129.1 %reduce-scatter.5.cloned.1.call-start = ((), (), s32[]{:S(2)}) async-start(), calls=%async_computation.4 | async-start | bytes 3932160 | tf_op jit(solution)/shard_map/reduce_scatter | solution.py:129
  468.9 59.9 %copy-start.2 = (bf16[256,1536]{1,0:T(8,128)(2,1)S(1)}, bf16[256,1536]{1,0:T(8,128)(2,1)}, u32[]{:S(2)}) copy-start(bf16[256,1536]{1,0:T(8,128)(2,1)} %copy-done.1) | copy-start | bytes 2359300
Sparse Core Ops, SparseCore 0:
  8.9 151.9 all-gather.8
  162.5 147.8 all-gather.10
  336.1 56.9 reduce-scatter.2
  399.8 43.4 all-gather.6
  469.0 59.6 reduce-scatter.4

commit v2 on v1

v2 whole, which is shorter than its diff:
```python
import functools

import jax
import jax.numpy as jnp
from jax import lax
from jax.experimental import pallas as pl
from jax.experimental.pallas import tpu as pltpu
from jax.sharding import PartitionSpec as P

FF = 24576


EPSILON = 1e-05
UNROLL = 4


def add_blocks(acc, source, weights, slots, counts, offset, d_blocks, f_blocks, into_hidden):
    cells, slot_count = weights.shape[0], weights.shape[1]
    step = UNROLL if slot_count % UNROLL == 0 else 1

    def cell_body(cell, carry):
        count = counts[offset + cell]

        def group(g, inner):
            products = []
            for j in range(step):
                n = g * step + j
                usable = n < count
                p = jnp.where(usable, slots[(offset + cell) * slot_count + n], 0)
                d = cell * d_blocks + lax.div(p, f_blocks)
                f = lax.rem(p, f_blocks)
                src, dst = (d, f) if into_hidden else (f, d)
                w = weights[cell, n]
                w = jnp.where(usable, w, jnp.zeros_like(w))
                products.append(
                    (dst, jnp.dot(source[src], w, preferred_element_type=jnp.float32))
                )
            for dst, value in products:
                acc[dst] += value
            return inner

        lax.fori_loop(0, lax.div(count + step - 1, step), group, 0)
        return carry

    lax.fori_loop(0, cells, cell_body, 0)


def clear_blocks(acc, count):
    def body(i, carry):
        acc[i] = jnp.zeros_like(acc[i])
        return carry

    lax.fori_loop(0, count, body, 0)


def hidden_kernel(d_blocks, f_blocks, active, slots, counts, x, gain, w_in, hidden, normed, acc):
    @pl.when(active[0] == 1)
    def _():
        cells = w_in.shape[0]
        all_d = cells * d_blocks
        blk = w_in.shape[-1]
        total = jnp.zeros((x.shape[0], 1), jnp.float32)
        for d in range(all_d):
            part = x[:, d * blk : (d + 1) * blk].astype(jnp.float32)
            total = total + jnp.sum(part * part, axis=1, keepdims=True)
        scale = lax.rsqrt(total / (all_d * blk) + EPSILON)
        for d in range(all_d):
            cols = slice(d * blk, (d + 1) * blk)
            normed[d] = (x[:, cols].astype(jnp.float32) * scale * gain[:, cols]).astype(jnp.bfloat16)
        clear_blocks(acc, f_blocks)
        add_blocks(acc, normed, w_in, slots, counts, 0, d_blocks, f_blocks, True)

        def activate(i, carry):
            hidden[i] = jax.nn.gelu(acc[i]).astype(jnp.bfloat16)
            return carry

        lax.fori_loop(0, f_blocks, activate, 0)


def part_kernel(d_blocks, f_blocks, active, slots, counts, hidden, w_out, out, acc):
    @pl.when(active[0] == 1)
    def _():
        cells = w_out.shape[0]
        all_d = cells * d_blocks
        blk = w_out.shape[-1]
        clear_blocks(acc, all_d)
        add_blocks(acc, hidden, w_out, slots, counts, cells, d_blocks, f_blocks, False)
        for d in range(all_d):
            out[:, d * blk : (d + 1) * blk] = acc[d].astype(jnp.bfloat16)


VMEM = pl.BlockSpec(memory_space=pltpu.VMEM)
SMEM = pl.BlockSpec(memory_space=pltpu.SMEM)


def cost(tokens, weights):
    return pl.CostEstimate(
        flops=2 * tokens * weights.size, bytes_accessed=2 * weights.size, transcendentals=0
    )


def hidden_call(active, slots, counts, x, gain, w_in, d_blocks, f_blocks):
    tokens, width = x.shape
    blk = w_in.shape[-1]
    return pl.pallas_call(
        functools.partial(hidden_kernel, d_blocks, f_blocks),
        out_shape=jax.ShapeDtypeStruct((f_blocks, tokens, blk), jnp.bfloat16),
        in_specs=[SMEM, SMEM, SMEM, VMEM, VMEM, VMEM],
        out_specs=VMEM,
        scratch_shapes=[
            pltpu.VMEM((width // blk, tokens, blk), jnp.bfloat16),
            pltpu.VMEM((f_blocks, tokens, blk), jnp.float32),
        ],
        compiler_params=pltpu.CompilerParams(vmem_limit_bytes=40 * 2**20),
        cost_estimate=cost(tokens, w_in),
    )(active, slots, counts, x, gain, w_in)


def part_call(active, slots, counts, hidden, w_out, d_blocks, f_blocks):
    tokens, blk = hidden.shape[1:]
    all_d = w_out.shape[0] * d_blocks
    return pl.pallas_call(
        functools.partial(part_kernel, d_blocks, f_blocks),
        out_shape=jax.ShapeDtypeStruct((tokens, all_d * blk), jnp.bfloat16),
        in_specs=[SMEM, SMEM, SMEM, VMEM, VMEM],
        out_specs=VMEM,
        scratch_shapes=[pltpu.VMEM((all_d, tokens, blk), jnp.float32)],
        compiler_params=pltpu.CompilerParams(vmem_limit_bytes=40 * 2**20),
        cost_estimate=cost(tokens, w_out),
    )(active, slots, counts, hidden, w_out)


def combine_kernel(phase, passes_on, part, current, *refs):
    if passes_on:
        result, full, landed, send_sem, recv_sem, push_sem, full_sem = refs
    else:
        result, landed, send_sem, recv_sem = refs
    cols = lax.axis_size("col")
    width = current.shape[1]
    mine = lax.axis_index("section")
    col = lax.axis_index("col")
    barrier = pltpu.get_barrier_semaphore()

    def device(section, other):
        return {"section": section, "col": other}

    def columns(c):
        return pl.ds(pl.multiple_of(c * width, width), width)

    def share(k):
        other = lax.rem(col + k, cols)
        return pltpu.make_async_remote_copy(
            src_ref=part.at[:, columns(other)],
            dst_ref=landed.at[k - 1],
            send_sem=send_sem.at[k - 1],
            recv_sem=recv_sem.at[k - 1],
            device_id=device(phase, other),
            device_id_type=pl.DeviceIdType.MESH,
        )

    def push(k):
        other = lax.rem(col + k, cols)
        return pltpu.make_async_remote_copy(
            src_ref=result,
            dst_ref=full.at[:, columns(col)],
            send_sem=push_sem.at[k],
            recv_sem=full_sem.at[k],
            device_id=device(phase + 1, other),
            device_id_type=pl.DeviceIdType.MESH,
        )

    @pl.when(mine == phase)
    def _():
        for k in range(1, cols):
            other = lax.rem(col + k, cols)
            pl.semaphore_signal(
                barrier, inc=1, device_id=device(phase, other), device_id_type=pl.DeviceIdType.MESH
            )
        if passes_on:
            for k in range(cols):
                other = lax.rem(col + k, cols)
                pl.semaphore_signal(
                    barrier, inc=1, device_id=device(phase + 1, other), device_id_type=pl.DeviceIdType.MESH
                )
        pl.semaphore_wait(barrier, 2 * cols - 1 if passes_on else cols - 1)
        shares = [share(k) for k in range(1, cols)]
        for copy in shares:
            copy.start()
        for copy in shares:
            copy.wait()
        total = part[:, columns(col)].astype(jnp.float32)
        for k in range(1, cols):
            total = total + landed[k - 1].astype(jnp.float32)
        result[...] = (current[...].astype(jnp.float32) + total).astype(jnp.bfloat16)
        if passes_on:
            pushes = [push(k) for k in range(cols)]
            for copy in pushes:
                copy.start()
            for copy in pushes:
                copy.wait_send()

    if passes_on:
        @pl.when(mine == phase + 1)
        def _():
            for k in range(cols):
                other = lax.rem(col + k, cols)
                pl.semaphore_signal(
                    barrier, inc=1, device_id=device(phase, other), device_id_type=pl.DeviceIdType.MESH
                )
            pl.semaphore_wait(barrier, cols)
            for k in range(cols):
                source = lax.rem(col + cols - k, cols)
                pltpu.make_async_remote_copy(
                    src_ref=result,
                    dst_ref=full.at[:, columns(source)],
                    send_sem=push_sem.at[k],
                    recv_sem=full_sem.at[k],
                    device_id=device(phase, source),
                    device_id_type=pl.DeviceIdType.MESH,
                ).wait_recv()


def combine(phase, passes_on, part, current):
    tokens, width = current.shape
    cols = part.shape[1] // width
    shapes = [jax.ShapeDtypeStruct(current.shape, jnp.bfloat16)]
    sems = [pltpu.SemaphoreType.DMA((cols,))] * 2
    if passes_on:
        shapes.append(jax.ShapeDtypeStruct(part.shape, jnp.bfloat16))
        sems = sems * 2
    return pl.pallas_call(
        functools.partial(combine_kernel, phase, passes_on),
        out_shape=shapes,
        in_specs=[VMEM, VMEM],
        out_specs=[VMEM] * len(shapes),
        scratch_shapes=[pltpu.VMEM((cols, tokens, width), jnp.bfloat16)] + sems,
        compiler_params=pltpu.CompilerParams(
            collective_id=phase, has_side_effects=True, vmem_limit_bytes=32 * 2**20
        ),
        cost_estimate=pl.CostEstimate(
            flops=part.size, bytes_accessed=16 * part.size, transcendentals=0
        ),
    )(part, current)


def shards(inputs, norm_gain, w_in, w_in_slot, w_in_count, w_out, w_out_slot, w_out_count):
    phase_idx = lax.axis_index("section")
    col_idx = lax.axis_index("col")
    col_total = lax.axis_size("col")
    row_total = lax.axis_size("row")
    micro_count, token_rows, model_width = inputs.shape
    shard_width = model_width // col_total
    blk = w_in.shape[-1]
    d_blocks = model_width // blk // row_total
    f_blocks = FF // blk // col_total
    slot_count = w_in.shape[3]
    own_in, own_out = w_in[0, 0, 0], w_out[0, 0, 0]
    sibling_out = lax.ppermute(own_out, "section", [(0, 1), (1, 0)])
    carried = [
        lax.all_gather(jnp.where(phase_idx == 0, own_in, sibling_out), "row", axis=0)
    ]
    meta = jnp.concatenate(
        [w_in_slot.reshape(-1), w_out_slot.reshape(-1), w_in_count.reshape(-1), w_out_count.reshape(-1)]
    )
    meta = lax.all_gather(meta, "row", axis=0)
    second, first, meta = lax.optimization_barrier(
        (jnp.where(phase_idx == 1, own_in, sibling_out), carried[0], meta)
    )
    carried = [first, lax.all_gather(second, "row", axis=0)]
    slots = jnp.concatenate(
        [meta[:, :slot_count].reshape(-1), meta[:, slot_count : 2 * slot_count].reshape(-1)]
    )
    counts = jnp.concatenate([meta[:, 2 * slot_count], meta[:, 2 * slot_count + 1]])
    tokens = micro_count * token_rows

    full = inputs.reshape(tokens, model_width)
    current = lax.dynamic_slice_in_dim(full, col_idx * shard_width, shard_width, 1)
    results = []
    for phase in range(2):
        active = (phase_idx == phase).astype(jnp.int32).reshape(1)
        out_weights = lax.ppermute(carried[phase], "section", [(1 - phase, phase)])
        hidden = hidden_call(active, slots, counts, full, norm_gain, carried[phase], d_blocks, f_blocks)
        part = part_call(active, slots, counts, hidden, out_weights, d_blocks, f_blocks)
        if phase == 0:
            result, full = combine(0, True, part, current)
            full, carried[1] = lax.optimization_barrier((full, carried[1]))
            current = lax.dynamic_slice_in_dim(full, col_idx * shard_width, shard_width, 1)
        else:
            [result] = combine(1, False, part, current)
        results.append(result)
    out = jnp.where(phase_idx == 0, results[0], results[1])
    return out.reshape(1, micro_count, token_rows, shard_width)


def solution(mesh):
    placed = (
        P(None, "row", None),
        P("section", None),
        P("section", "row", "col", None, None, None),
        P("section", "row", "col", None),
        P("section", "row", "col"),
        P("section", "row", "col", None, None, None),
        P("section", "row", "col", None),
        P("section", "row", "col"),
    )
    return jax.shard_map(
        shards,
        mesh=mesh,
        in_specs=placed,
        out_specs=P("section", None, "row", "col"),
        check_vma=False,
    )
```

time: 532 us -> 380 us (0.71)
  waiting for transfers between devices: 456 us -> 222 us
  Pallas kernels: 51.1 us -> 121 us
  starting transfers between devices: 1.48 us -> 6.96 us
    all_gather x3 -> x2, waiting for transfers between devices: 335 us -> 214 us  [the longest x1 141 us: shards(): lax.all_gather(jnp.where(phase_idx == 0, own_in, sibling_out), 'row', axi...]
    reduce_scatter x2 -> x0, waiting for transfers between devices: 117 us -> none  [shards(): branch = lax.psum_scatter(part, 'col', scatter_dimension=1, tiled=True)]
    pallas_call x2 -> x6, Pallas kernels: 51.1 us -> 121 us  [the longest x2 83.4 us: combine(): pl.pallas_call(functools.partial(combine_kernel, phase, passes_on), out_s...]
    ppermute x1 -> x3, starting transfers between devices: 1.29 us -> 6.92 us  [the longest x2 6.86 us: shards(): out_weights = lax.ppermute(carried[phase], 'section', [(1 - phase, phase)])]
    ppermute x1 -> x3, waiting for transfers between devices: 2.88 us -> 8.33 us  [the longest x1 4.31 us: shards(): sibling_out = lax.ppermute(own_out, 'section', [(0, 1), (1, 0)])]
  transfers between devices with their start and end apart: 6 -> 5, of which waited for: 6 -> 4; matrix products, arithmetic and copies ran while one was open for 0% -> 1% of each run, Pallas kernels for 0% -> 21%
where the time goes in v2:
time: 380 us; the launch traced here: 381 us
  waiting for transfers between devices  222 us (58%)
  Pallas kernels  121 us (32%)
  between operations  15.8 us (4%)
  blocking collectives  7.56 us (2%)
  starting transfers between devices  6.96 us (2%)
  other arithmetic  5.22 us (1%)
    all_gather x1, waiting for transfers between devices, shards(): lax.all_gather(jnp.where(phase_idx == 0, own_in, sibling_out), 'row', axi...  141 us
    pallas_call x2, Pallas kernels, combine(): pl.pallas_call(functools.partial(combine_kernel, phase, passes_on), out_s...  83.4 us
    all_gather x1, waiting for transfers between devices, shards(): carried = [first, lax.all_gather(second, 'row', axis=0)]  72.1 us
    pallas_call x2, Pallas kernels, part_call(): pl.pallas_call(functools.partial(part_kernel, d_blocks, f_blocks), out_sh...  18.6 us
    pallas_call x2, Pallas kernels, hidden_call(): pl.pallas_call(functools.partial(hidden_kernel, d_blocks, f_blocks), out_...  18.5 us
  transfers between devices with their start and end apart: 5, of which 4 were waited for; matrix products, arithmetic and copies ran while one was open for 1% of the time, Pallas kernels for 21%

profile of v2, /device:TPU:1, one launch (start us, length us, event | category | flops | bytes accessed | tf_op | source)
XLA Modules:
  0.0 380.9 jit_solution(2317036836329651029)
XLA Ops:
  6.6 4.3 %collective-permute-done = bf16[64,128,128]{2,1,0:T(8,128)(2,1)S(1)} collective-permute-done((bf16[64,128,128]{2,1,0:T(8,128)(2,1)}, bf16[64,128,128]{2,1,0:T(8,128)(2,1)S(1)}, u32[]{:S(2)}, u32[]{:S(2)}) %collective-permute-start) | collective-permute-done | bytes 2097184 | tf_op jit(solution)/shard_map/ppermute | solution.py:258
  10.9 4.0 %bitcast_select_fusion = (bf16[64,128,128]{2,1,0:T(8,128)(2,1)}, bf16[64,128,128]{2,1,0:T(8,128)(2,1)}) fusion(bf16[64,128,128]{2,1,0:T(8,128)(2,1)S(1)} %collective-permute-done, bf16[1,1,1,64,128,128]{5,4,3,2,1,0:T(8,128)(2,1)} %param.10, pred[]{:T(512)S(6)} %eq.4, pred[]{:T(512)S(6)} %eq.10), kind=kLoop, calls=%fused_computation | loop fusion | flops 2097152 | bytes 8388610 | tf_op jit(solution)/shard_map/jit(_where)/select_n | solution.py:260
  16.5 0.6 dynamic-slice
  17.8 0.2 add_dynamic-update-slice_fusion
  18.0 7.6 %all-reduce = s32[520]{0:T(1024)S(1)} all-reduce(s32[520]{0:T(1024)S(1)} %add_dynamic-update-slice_fusion), channel_id=3, replica_groups=mesh['section'=2,'row'=4,'col'=4] {'row'}, use_global_device_ids=true, to_apply=%add | all-reduce | flops 520 | bytes 4160
  25.6 0.1 reshape.51
  25.6 141.4 %all-gather.6.cloned.1.call-done = bf16[256,128,128]{2,1,0:T(8,128)(2,1)} async-done(((bf16[64,128,128]{2,1,0:T(8,128)(2,1)}), bf16[256,128,128]{2,1,0:T(8,128)(2,1)}) %all-gather.6.cloned.1.call-update) | async-done | bytes 8388624 | tf_op jit(solution)/shard_map/all_gather | solution.py:260
  167.1 5.6 %collective-permute-start.1 = (bf16[4,64,128,128]{3,2,1,0:T(8,128)(2,1)}, bf16[4,64,128,128]{3,2,1,0:T(8,128)(2,1)}, u32[]{:S(2)}, u32[]{:S(2)}) collective-permute-start(bf16[4,64,128,128]{3,2,1,0:T(8,128)(2,1)} %bitcast.19), channel_id=1, source_target_pairs={{16,0},{17,1},{18,2},{19,3},{20,4},{21,5},{22,6},{23,7},{24,8},{25... | collective-permute-start | bytes 25165832 | tf_op jit(solution)/shard_map/ppermute | solution.py:281
  172.6 0.9 constant_dynamic-slice_fusion.1.current
  173.6 0.1 reshape.40
  173.7 0.1 reshape.41
  173.8 0.2 slice_reduce_fusion.1
  174.0 0.1 pad_add_fusion.counts
  174.1 4.4 %shard_map.82.hidden = bf16[48,256,128]{2,1,0:T(8,128)(2,1)S(1)} custom-call(s32[1]{0:T(128)} %bitcast.active, s32[512]{0:T(512)S(1)} %constant_dynamic-update-slice_fusion.slots, s32[8]{0:T(128)S(1)} %pad_add_fusion.counts, bf16[256,6144]{1,0:T(8,128)(2,1)S(1)} %bitcast.18, f32[1,6144]{1,0:T(1,128)S(1)} %copy-done.4, bf16[4,64,128,128]{3,2,1,0:T(8,128)(2,1)} %bitcast.20), custom_call_target="tpu_custom_call" | custom-call | flops 2147483648 | bytes 8388608 | tf_op jit(solution)/shard_map/pallas_call | solution.py:105
  178.5 4.0 %collective-permute-done.1.w_out = bf16[4,64,128,128]{3,2,1,0:T(8,128)(2,1)} collective-permute-done((bf16[4,64,128,128]{3,2,1,0:T(8,128)(2,1)}, bf16[4,64,128,128]{3,2,1,0:T(8,128)(2,1)}, u32[]{:S(2)}, u32[]{:S(2)}) %collective-permute-start.1) | collective-permute-done | bytes 8388640 | tf_op jit(solution)/shard_map/ppermute | solution.py:281
  182.5 3.4 shard_map.83.part
  185.9 57.5 %shard_map.84 = (bf16[256,1536]{1,0:T(8,128)(2,1)S(1)}, bf16[256,6144]{1,0:T(8,128)(2,1)S(1)}) custom-call(bf16[256,6144]{1,0:T(8,128)(2,1)S(1)} %shard_map.83.part, bf16[256,1536]{1,0:T(8,128)(2,1)S(1)} %copy-done.1), custom_call_target="tpu_custom_call" | custom-call | flops 1572864 | bytes 25165824 | tf_op jit(solution)/shard_map/pallas_call | solution.py:231
  243.5 0.9 copy-done.2
  244.3 72.1 %all-gather.8.cloned.1.call-done = bf16[256,128,128]{2,1,0:T(8,128)(2,1)} async-done(((bf16[64,128,128]{2,1,0:T(8,128)(2,1)}), bf16[256,128,128]{2,1,0:T(8,128)(2,1)}) %all-gather.8.cloned.1.call-update) | async-done | bytes 8388624 | tf_op jit(solution)/shard_map/all_gather | solution.py:269
  316.5 1.3 collective-permute-start.2
  317.8 14.1 %shard_map.85.hidden = bf16[48,256,128]{2,1,0:T(8,128)(2,1)S(1)} custom-call(s32[1]{0:T(128)} %bitcast.10.active, s32[512]{0:T(512)S(1)} %constant_dynamic-update-slice_fusion.slots, s32[8]{0:T(128)S(1)} %pad_add_fusion.counts, bf16[256,6144]{1,0:T(8,128)(2,1)S(1)} %get-tuple-element.17.x, f32[1,6144]{1,0:T(1,128)S(1)} %copy-done.4, ...), custom_call_target="tpu_custom_call" | custom-call | flops 2147483648 | bytes 8388608 | tf_op jit(solution)/shard_map/pallas_call | solution.py:105
  332.0 15.2 %shard_map.86.part = bf16[256,6144]{1,0:T(8,128)(2,1)S(1)} custom-call(s32[1]{0:T(128)} %bitcast.10.active, s32[512]{0:T(512)S(1)} %constant_dynamic-update-slice_fusion.slots, s32[8]{0:T(128)S(1)} %pad_add_fusion.counts, bf16[48,256,128]{2,1,0:T(8,128)(2,1)S(1)} %shard_map.85.hidden, bf16[4,64,128,128]{3,2,1,0:T(8,128)(2,1)} %collective-permute-done.2.w_out), custom_call_target="tpu_custom_call" | custom-call | flops 2147483648 | bytes 8388608 | tf_op jit(solution)/shard_map/pallas_call | solution.py:122
  347.2 25.9 %shard_map.87 = bf16[256,1536]{1,0:T(8,128)(2,1)S(1)} custom-call(bf16[256,6144]{1,0:T(8,128)(2,1)S(1)} %shard_map.86.part, bf16[256,1536]{1,0:T(8,128)(2,1)S(1)} %constant_dynamic-slice_fusion.current), custom_call_target="tpu_custom_call" | custom-call | flops 1572864 | bytes 25165824 | tf_op jit(solution)/shard_map/pallas_call | solution.py:231
  373.1 1.0 broadcast_select_fusion
  (27 shorter events, 0.3 us)
Async XLA Ops:
  6.5 160.5 %all-gather.6.cloned.1.call-start = ((), (), s32[]{:S(2)}) async-start(), calls=%async_computation | async-start | bytes 10485760 | tf_op jit(solution)/shard_map/all_gather | solution.py:260
  6.5 4.4 %collective-permute-start = (bf16[64,128,128]{2,1,0:T(8,128)(2,1)}, bf16[64,128,128]{2,1,0:T(8,128)(2,1)S(1)}, u32[]{:S(2)}, u32[]{:S(2)}) collective-permute-start(bf16[64,128,128]{2,1,0:T(8,128)(2,1)} %bitcast.25), channel_id=1, source_target_pairs={{0,16},{16,0},{1,17},{17,1},{2,18},{18,2},{3,19},{19,3},{4,20},{20... | collective-permute-start | bytes 6291464 | tf_op jit(solution)/shard_map/ppermute | solution.py:258
  6.6 9.9 %copy-start.7 = (u32[32]{0:T(128)S(1)}, u32[32]{0:T(128)}, u32[]{:S(2)}) copy-start(u32[32]{0:T(128)} %constant.27) | copy-start | bytes 388
  6.6 11.2 %copy-start.5 = (s32[1,1,1,64]{3,2,1,0:T(1,128)S(1)}, s32[1,1,1,64]{3,2,1,0:T(1,128)}, u32[]{:S(2)}) copy-start(s32[1,1,1,64]{3,2,1,0:T(1,128)} %param.14) | copy-start | bytes 772
  6.6 11.2 %copy-start.6 = (s32[1,1,1,64]{3,2,1,0:T(1,128)S(1)}, s32[1,1,1,64]{3,2,1,0:T(1,128)}, u32[]{:S(2)}) copy-start(s32[1,1,1,64]{3,2,1,0:T(1,128)} %param.11) | copy-start | bytes 772
  14.9 157.7 %copy-start = (bf16[2,128,6144]{2,1,0:T(8,128)(2,1)S(1)}, bf16[2,128,6144]{2,1,0:T(8,128)(2,1)}, u32[]{:S(2)}) copy-start(bf16[2,128,6144]{2,1,0:T(8,128)(2,1)} %param.8) | copy-start | bytes 9437188
  14.9 159.2 %copy-start.4 = (f32[1,6144]{1,0:T(1,128)S(1)}, f32[1,6144]{1,0:T(1,128)}, u32[]{:S(2)}) copy-start(f32[1,6144]{1,0:T(1,128)} %gain.3) | copy-start | bytes 73732
  14.9 301.6 %all-gather.8.cloned.1.call-start = ((), (), s32[]{:S(2)}) async-start(), calls=%async_computation.1 | async-start | bytes 10485760 | tf_op jit(solution)/shard_map/all_gather | solution.py:269
  167.1 15.5 %collective-permute-start.1 = (bf16[4,64,128,128]{3,2,1,0:T(8,128)(2,1)}, bf16[4,64,128,128]{3,2,1,0:T(8,128)(2,1)}, u32[]{:S(2)}, u32[]{:S(2)}) collective-permute-start(bf16[4,64,128,128]{3,2,1,0:T(8,128)(2,1)} %bitcast.19), channel_id=1, source_target_pairs={{16,0},{17,1},{18,2},{19,3},{20,4},{21,5},{22,6},{23,7},{24,8},{25... | collective-permute-start | bytes 25165832 | tf_op jit(solution)/shard_map/ppermute | solution.py:281
  178.5 7.4 %copy-start.1 = (bf16[256,1536]{1,0:T(8,128)(2,1)S(1)}, bf16[256,1536]{1,0:T(8,128)(2,1)}, u32[]{:S(2)}) copy-start(bf16[256,1536]{1,0:T(8,128)(2,1)} %constant_dynamic-slice_fusion.1.current) | copy-start | bytes 2359300
  243.5 0.9 copy-start.2
  316.5 15.5 %collective-permute-start.2 = (bf16[4,64,128,128]{3,2,1,0:T(8,128)(2,1)}, bf16[4,64,128,128]{3,2,1,0:T(8,128)(2,1)}, u32[]{:S(2)}, u32[]{:S(2)}) collective-permute-start(bf16[4,64,128,128]{3,2,1,0:T(8,128)(2,1)} %bitcast.21), channel_id=1, source_target_pairs={{0,16},{1,17},{2,18},{3,19},{4,20},{5,21},{6,22},{7,23},{8,24},{9,... | collective-permute-start | bytes 25165832 | tf_op jit(solution)/shard_map/ppermute | solution.py:281
  347.2 26.0 %copy-start.3 = (bf16[256,1536]{1,0:T(8,128)(2,1)S(1)}, bf16[256,1536]{1,0:T(8,128)(2,1)}, u32[]{:S(2)}) copy-start(bf16[256,1536]{1,0:T(8,128)(2,1)} %copy-done.2) | copy-start | bytes 2359300
Sparse Core Ops, SparseCore 0:
  15.1 151.9 all-gather.5
  168.6 147.8 all-gather.7

commit v3 on v2

--- a/solution.py
+++ b/solution.py
@@ -1,4 +1,5 @@
 import functools
+import math
 
 import jax
 import jax.numpy as jnp
@@ -11,22 +12,23 @@
 
 
 EPSILON = 1e-05
-UNROLL = 4
-
-
-def add_blocks(acc, source, weights, slots, counts, offset, d_blocks, f_blocks, into_hidden):
-    cells, slot_count = weights.shape[0], weights.shape[1]
-    step = UNROLL if slot_count % UNROLL == 0 else 1
+UNROLL = 8
+
+
+def add_blocks(acc, source, weights, slots, counts, base, offset, d_blocks, f_blocks, into_hidden):
+    cells, held = weights.shape[0], weights.shape[1]
+    slot_count = slots.shape[0] // (2 * cells)
+    step = math.gcd(UNROLL, held)
 
     def cell_body(cell, carry):
-        count = counts[offset + cell]
+        count = jnp.clip(counts[offset + cell] - base, 0, held)
 
         def group(g, inner):
             products = []
             for j in range(step):
                 n = g * step + j
                 usable = n < count
-                p = jnp.where(usable, slots[(offset + cell) * slot_count + n], 0)
+                p = jnp.where(usable, slots[(offset + cell) * slot_count + base + n], 0)
                 d = cell * d_blocks + lax.div(p, f_blocks)
                 f = lax.rem(p, f_blocks)
                 src, dst = (d, f) if into_hidden else (f, d)
@@ -53,7 +55,17 @@
     lax.fori_loop(0, count, body, 0)
 
 
-def hidden_kernel(d_blocks, f_blocks, active, slots, counts, x, gain, w_in, hidden, normed, acc):
+def add_all(acc, source, pieces, slots, counts, offset, d_blocks, f_blocks, into_hidden):
+    base = 0
+    for piece in pieces:
+        add_blocks(acc, source, piece, slots, counts, base, offset, d_blocks, f_blocks, into_hidden)
+        base += piece.shape[1]
+
+
+def hidden_kernel(d_blocks, f_blocks, active, slots, counts, x, gain, *refs):
+    *pieces, hidden, normed, acc = refs
+    w_in = pieces[0]
+
     @pl.when(active[0] == 1)
     def _():
         cells = w_in.shape[0]
@@ -68,7 +80,7 @@
             cols = slice(d * blk, (d + 1) * blk)
             normed[d] = (x[:, cols].astype(jnp.float32) * scale * gain[:, cols]).astype(jnp.bfloat16)
         clear_blocks(acc, f_blocks)
-        add_blocks(acc, normed, w_in, slots, counts, 0, d_blocks, f_blocks, True)
+        add_all(acc, normed, pieces, slots, counts, 0, d_blocks, f_blocks, True)
 
         def activate(i, carry):
             hidden[i] = jax.nn.gelu(acc[i]).astype(jnp.bfloat16)
@@ -77,14 +89,17 @@
         lax.fori_loop(0, f_blocks, activate, 0)
 
 
-def part_kernel(d_blocks, f_blocks, active, slots, counts, hidden, w_out, out, acc):
+def part_kernel(d_blocks, f_blocks, active, slots, counts, hidden, *refs):
+    *pieces, out, acc = refs
+    w_out = pieces[0]
+
     @pl.when(active[0] == 1)
     def _():
         cells = w_out.shape[0]
         all_d = cells * d_blocks
         blk = w_out.shape[-1]
         clear_blocks(acc, all_d)
-        add_blocks(acc, hidden, w_out, slots, counts, cells, d_blocks, f_blocks, False)
+        add_all(acc, hidden, pieces, slots, counts, cells, d_blocks, f_blocks, False)
         for d in range(all_d):
             out[:, d * blk : (d + 1) * blk] = acc[d].astype(jnp.bfloat16)
 
@@ -93,41 +108,42 @@
 SMEM = pl.BlockSpec(memory_space=pltpu.SMEM)
 
 
-def cost(tokens, weights):
+def cost(tokens, pieces):
+    size = sum(piece.size for piece in pieces)
     return pl.CostEstimate(
-        flops=2 * tokens * weights.size, bytes_accessed=2 * weights.size, transcendentals=0
-    )
-
-
-def hidden_call(active, slots, counts, x, gain, w_in, d_blocks, f_blocks):
+        flops=2 * tokens * size, bytes_accessed=2 * size, transcendentals=0
+    )
+
+
+def hidden_call(active, slots, counts, x, gain, pieces, d_blocks, f_blocks):
     tokens, width = x.shape
-    blk = w_in.shape[-1]
+    blk = pieces[0].shape[-1]
     return pl.pallas_call(
         functools.partial(hidden_kernel, d_blocks, f_blocks),
         out_shape=jax.ShapeDtypeStruct((f_blocks, tokens, blk), jnp.bfloat16),
-        in_specs=[SMEM, SMEM, SMEM, VMEM, VMEM, VMEM],
+        in_specs=[SMEM, SMEM, SMEM, VMEM, VMEM] + [VMEM] * len(pieces),
         out_specs=VMEM,
         scratch_shapes=[
             pltpu.VMEM((width // blk, tokens, blk), jnp.bfloat16),
             pltpu.VMEM((f_blocks, tokens, blk), jnp.float32),
         ],
         compiler_params=pltpu.CompilerParams(vmem_limit_bytes=40 * 2**20),
-        cost_estimate=cost(tokens, w_in),
-    )(active, slots, counts, x, gain, w_in)
-
-
-def part_call(active, slots, counts, hidden, w_out, d_blocks, f_blocks):
+        cost_estimate=cost(tokens, pieces),
+    )(active, slots, counts, x, gain, *pieces)
+
+
+def part_call(active, slots, counts, hidden, pieces, d_blocks, f_blocks):
     tokens, blk = hidden.shape[1:]
-    all_d = w_out.shape[0] * d_blocks
+    all_d = pieces[0].shape[0] * d_blocks
     return pl.pallas_call(
         functools.partial(part_kernel, d_blocks, f_blocks),
         out_shape=jax.ShapeDtypeStruct((tokens, all_d * blk), jnp.bfloat16),
-        in_specs=[SMEM, SMEM, SMEM, VMEM, VMEM],
+        in_specs=[SMEM, SMEM, SMEM, VMEM] + [VMEM] * len(pieces),
         out_specs=VMEM,
         scratch_shapes=[pltpu.VMEM((all_d, tokens, blk), jnp.float32)],
         compiler_params=pltpu.CompilerParams(vmem_limit_bytes=40 * 2**20),
-        cost_estimate=cost(tokens, w_out),
-    )(active, slots, counts, hidden, w_out)
+        cost_estimate=cost(tokens, pieces),
+    )(active, slots, counts, hidden, *pieces)
 
 
 def combine_kernel(phase, passes_on, part, current, *refs):
@@ -255,18 +271,23 @@
     f_blocks = FF // blk // col_total
     slot_count = w_in.shape[3]
     own_in, own_out = w_in[0, 0, 0], w_out[0, 0, 0]
-    sibling_out = lax.ppermute(own_out, "section", [(0, 1), (1, 0)])
-    carried = [
-        lax.all_gather(jnp.where(phase_idx == 0, own_in, sibling_out), "row", axis=0)
-    ]
+    half = slot_count // 2
+    first_out = lax.ppermute(own_out, "section", [(0, 1)])
+    upper = lax.ppermute(jnp.concatenate([own_in[half:], own_out[half:]]), "section", [(1, 0)])
+    first = lax.all_gather(jnp.where(phase_idx == 0, own_in, first_out), "row", axis=0)
     meta = jnp.concatenate(
         [w_in_slot.reshape(-1), w_out_slot.reshape(-1), w_in_count.reshape(-1), w_out_count.reshape(-1)]
     )
     meta = lax.all_gather(meta, "row", axis=0)
-    second, first, meta = lax.optimization_barrier(
-        (jnp.where(phase_idx == 1, own_in, sibling_out), carried[0], meta)
-    )
-    carried = [first, lax.all_gather(second, "row", axis=0)]
+    second, third, first, meta = lax.optimization_barrier(
+        (
+            jnp.where(phase_idx == 1, own_in[:half], upper[: slot_count - half]),
+            jnp.where(phase_idx == 1, own_out[:half], upper[slot_count - half :]),
+            first,
+            meta,
+        )
+    )
+    second = lax.all_gather(second, "row", axis=0)
     slots = jnp.concatenate(
         [meta[:, :slot_count].reshape(-1), meta[:, slot_count : 2 * slot_count].reshape(-1)]
     )
@@ -275,20 +296,24 @@
 
     full = inputs.reshape(tokens, model_width)
     current = lax.dynamic_slice_in_dim(full, col_idx * shard_width, shard_width, 1)
-    results = []
-    for phase in range(2):
-        active = (phase_idx == phase).astype(jnp.int32).reshape(1)
-        out_weights = lax.ppermute(carried[phase], "section", [(1 - phase, phase)])
-        hidden = hidden_call(active, slots, counts, full, norm_gain, carried[phase], d_blocks, f_blocks)
-        part = part_call(active, slots, counts, hidden, out_weights, d_blocks, f_blocks)
-        if phase == 0:
-            result, full = combine(0, True, part, current)
-            full, carried[1] = lax.optimization_barrier((full, carried[1]))
-            current = lax.dynamic_slice_in_dim(full, col_idx * shard_width, shard_width, 1)
-        else:
-            [result] = combine(1, False, part, current)
-        results.append(result)
-    out = jnp.where(phase_idx == 0, results[0], results[1])
+    sizes = (d_blocks, f_blocks)
+    active = (phase_idx == 0).astype(jnp.int32).reshape(1)
+    out_weights = lax.ppermute(first, "section", [(1, 0)])
+    hidden = hidden_call(active, slots, counts, full, norm_gain, [first], *sizes)
+    part = part_call(active, slots, counts, hidden, [out_weights], *sizes)
+    earlier, full = combine(0, True, part, current)
+
+    full, second, third = lax.optimization_barrier((full, second, third))
+    third = lax.all_gather(third, "row", axis=0)
+    active = (phase_idx == 1).astype(jnp.int32).reshape(1)
+    current = lax.dynamic_slice_in_dim(full, col_idx * shard_width, shard_width, 1)
+    rest = lax.ppermute(second, "section", [(0, 1)])
+    hidden = hidden_call(active, slots, counts, full, norm_gain, [second, rest], *sizes)
+    hidden, third = lax.optimization_barrier((hidden, third))
+    rest = lax.ppermute(third, "section", [(0, 1)])
+    part = part_call(active, slots, counts, hidden, [third, rest], *sizes)
+    [later] = combine(1, False, part, current)
+    out = jnp.where(phase_idx == 0, earlier, later)
     return out.reshape(1, micro_count, token_rows, shard_width)
 
 

time: 380 us -> 385 us (1.013)
  Pallas kernels: 121 us -> 104 us
  local copies, waits for them, and re-layouts: 3.01 us -> 16.3 us
  waiting for transfers between devices: 222 us -> 214 us
  starting transfers between devices: 6.96 us -> 12.9 us
  blocking collectives: 7.56 us -> 12.3 us
  other arithmetic: 5.22 us -> 9.83 us
    all_gather x2 -> x3, waiting for transfers between devices: 214 us -> 189 us  [the longest x1 126 us: shards(): lax.all_gather(jnp.where(phase_idx == 0, own_in, first_out), 'row', axis=0)]
    ppermute x3 -> x5, waiting for transfers between devices: 8.33 us -> 24.6 us  [the longest x1 8.1 us: shards(): rest = lax.ppermute(second, 'section', [(0, 1)])]
    unnamed x19 -> x31, local copies, waits for them, and re-layouts: 1.51 us -> 12.1 us
    pallas_call x2, Pallas kernels: 83.4 us -> 75.9 us  [combine(): pl.pallas_call(functools.partial(combine_kernel, phase, passes_on), out_s...]
    pallas_call x2, Pallas kernels: 18.6 us -> 12.5 us  [part_call(): pl.pallas_call(functools.partial(part_kernel, d_blocks, f_blocks), out_sh...]
    ppermute x3 -> x5, starting transfers between devices: 6.92 us -> 12.8 us  [the longest x1 5.57 us: shards(): out_weights = lax.ppermute(first, 'section', [(1, 0)])]
    unnamed x1, blocking collectives: 7.56 us -> 12.3 us
    select_n x2 -> x3, other arithmetic: 4.96 us -> 8.06 us  [the longest x1 3.89 us: shards(): jnp.where(phase_idx == 1, own_out[:half], upper[slot_count - half:])]
  transfers between devices with their start and end apart: 5 -> 8, of which waited for: 4 -> 7; matrix products, arithmetic and copies ran while one was open for 1% -> 3% of each run, Pallas kernels for 21% -> 19%
where the time goes in v3:
time: 385 us
  waiting for transfers between devices  214 us (56%)
  Pallas kernels  104 us (27%)
  local copies, waits for them, and re-layouts  16.3 us (4%)
  between operations  15.3 us (4%)
  starting transfers between devices  12.9 us (3%)
  blocking collectives  12.3 us (3%)
  other arithmetic  9.83 us (3%)
    all_gather x1, waiting for transfers between devices, shards(): lax.all_gather(jnp.where(phase_idx == 0, own_in, first_out), 'row', axis=0)  126 us
    pallas_call x2, Pallas kernels, combine(): pl.pallas_call(functools.partial(combine_kernel, phase, passes_on), out_s...  75.9 us
    all_gather x1, waiting for transfers between devices, shards(): third = lax.all_gather(third, 'row', axis=0)  54.6 us
    pallas_call x2, Pallas kernels, hidden_call(): pl.pallas_call(functools.partial(hidden_kernel, d_blocks, f_blocks), out_...  16 us
    pallas_call x2, Pallas kernels, part_call(): pl.pallas_call(functools.partial(part_kernel, d_blocks, f_blocks), out_sh...  12.5 us
    unnamed x1, blocking collectives  12.3 us
    unnamed x31, local copies, waits for them, and re-layouts  12.1 us
    all_gather x1, waiting for transfers between devices, shards(): second = lax.all_gather(second, 'row', axis=0)  8.76 us
  transfers between devices with their start and end apart: 8, of which 7 were waited for; matrix products, arithmetic and copies ran while one was open for 3% of the time, Pallas kernels for 19%

profile of v3, /device:TPU:1, one launch (start us, length us, event | category | flops | bytes accessed | tf_op | source)
XLA Modules:
  0.0 385.0 jit_solution(12749097207833587212)
XLA Ops:
  7.8 5.0 %collective-permute-done.1 = bf16[64,128,128]{2,1,0:T(8,128)(2,1)S(1)} collective-permute-done((bf16[64,128,128]{2,1,0:T(8,128)(2,1)}, bf16[64,128,128]{2,1,0:T(8,128)(2,1)S(1)}, u32[]{:S(2)}, u32[]{:S(2)}) %collective-permute-start.1) | collective-permute-done | bytes 2097184 | tf_op jit(solution)/shard_map/ppermute | solution.py:275
  12.8 3.2 bitcast_select_fusion
  18.0 1.5 pad_maximum_fusion
  19.5 3.4 collective-permute-start
  25.7 12.3 %all-reduce = s32[520]{0:T(1024)S(1)} all-reduce(s32[520]{0:T(1024)S(1)} %add_dynamic-update-slice_fusion), channel_id=3, replica_groups=mesh['section'=2,'row'=4,'col'=4] {'row'}, use_global_device_ids=true, to_apply=%add | all-reduce | flops 520 | bytes 4160
  38.0 3.9 %slice_select_fusion = (bf16[32,128,128]{2,1,0:T(8,128)(2,1)}, bf16[32,128,128]{2,1,0:T(8,128)(2,1)}) fusion(bf16[64,128,128]{2,1,0:T(8,128)(2,1)} %collective-permute-done, bf16[1,1,1,64,128,128]{5,4,3,2,1,0:T(8,128)(2,1)} %param.13, pred[]{:T(512)S(6)} %eq.5, bf16[1,1,1,64,128,128]{5,4,3,2,1,0:T(8,128)(2,1)} %param.10), kind=kLoop, calls=%fused_computation.2 | loop fusion | flops 1048576 | bytes 6291457 | tf_op jit(solution)/shard_map/jit(_where)/select_n | solution.py:285
  41.9 125.9 %all-gather.8.cloned.1.call-done = bf16[256,128,128]{2,1,0:T(8,128)(2,1)} async-done(((bf16[64,128,128]{2,1,0:T(8,128)(2,1)}), bf16[256,128,128]{2,1,0:T(8,128)(2,1)}) %all-gather.8.cloned.1.call-update) | async-done | bytes 8388624 | tf_op jit(solution)/shard_map/all_gather | solution.py:277
  167.8 5.6 %collective-permute-start.2 = (bf16[4,64,128,128]{3,2,1,0:T(8,128)(2,1)}, bf16[4,64,128,128]{3,2,1,0:T(8,128)(2,1)}, u32[]{:S(2)}, u32[]{:S(2)}) collective-permute-start(bf16[4,64,128,128]{3,2,1,0:T(8,128)(2,1)} %bitcast.31), channel_id=1, source_target_pairs={{16,0},{17,1},{18,2},{19,3},{20,4},{21,5},{22,6},{23,7},{24,8},{25... | collective-permute-start | bytes 25165832 | tf_op jit(solution)/shard_map/ppermute | solution.py:301
  174.9 3.5 shard_map.82.hidden
  178.5 4.8 %collective-permute-done.2.refs_0_ = bf16[4,64,128,128]{3,2,1,0:T(8,128)(2,1)} collective-permute-done((bf16[4,64,128,128]{3,2,1,0:T(8,128)(2,1)}, bf16[4,64,128,128]{3,2,1,0:T(8,128)(2,1)}, u32[]{:S(2)}, u32[]{:S(2)}) %collective-permute-start.2) | collective-permute-done | bytes 8388640 | tf_op jit(solution)/shard_map/ppermute | solution.py:301
  183.3 3.4 shard_map.83.part
  186.7 53.9 %shard_map.84 = (bf16[256,1536]{1,0:T(8,128)(2,1)S(1)}, bf16[256,6144]{1,0:T(8,128)(2,1)S(1)}) custom-call(bf16[256,6144]{1,0:T(8,128)(2,1)S(1)} %shard_map.83.part, bf16[256,1536]{1,0:T(8,128)(2,1)S(1)} %copy-done.5), custom_call_target="tpu_custom_call" | custom-call | flops 1572864 | bytes 25165824 | tf_op jit(solution)/shard_map/pallas_call | solution.py:247
  240.6 1.7 copy-done.1
  243.2 8.8 %all-gather.10.cloned.1.call-done = bf16[128,128,128]{2,1,0:T(8,128)(2,1)} async-done(((bf16[32,128,128]{2,1,0:T(8,128)(2,1)}), bf16[128,128,128]{2,1,0:T(8,128)(2,1)}) %all-gather.10.cloned.1.call-update) | async-done | bytes 4194320 | tf_op jit(solution)/shard_map/all_gather | solution.py:290
  253.3 8.1 %collective-permute-done.3.refs_1_ = bf16[4,32,128,128]{3,2,1,0:T(8,128)(2,1)} collective-permute-done((bf16[4,32,128,128]{3,2,1,0:T(8,128)(2,1)}, bf16[4,32,128,128]{3,2,1,0:T(8,128)(2,1)}, u32[]{:S(2)}, u32[]{:S(2)}) %collective-permute-start.3) | collective-permute-done | bytes 4194336 | tf_op jit(solution)/shard_map/ppermute | solution.py:310
  261.4 2.2 copy-done.2
  263.6 2.2 copy-done.3
  265.8 12.5 %shard_map.85.hidden = bf16[48,256,128]{2,1,0:T(8,128)(2,1)S(1)} custom-call(s32[1]{0:T(128)} %bitcast.14.active, s32[512]{0:T(512)S(1)} %constant_dynamic-update-slice_fusion.slots, s32[8]{0:T(128)S(1)} %pad_add_fusion.counts, bf16[256,6144]{1,0:T(8,128)(2,1)S(1)} %copy-done.2, f32[1,6144]{1,0:T(1,128)S(1)} %copy-done.8, ...), custom_call_target="tpu_custom_call" | custom-call | flops 2147483648 | bytes 8388608 | tf_op jit(solution)/shard_map/pallas_call | solution.py:121
  278.2 54.6 %all-gather.12.cloned.1.call-done = bf16[128,128,128]{2,1,0:T(8,128)(2,1)} async-done(((bf16[32,128,128]{2,1,0:T(8,128)(2,1)}), bf16[128,128,128]{2,1,0:T(8,128)(2,1)}) %all-gather.12.cloned.1.call-update) | async-done | bytes 4194320 | tf_op jit(solution)/shard_map/all_gather | solution.py:307
  335.4 6.8 %collective-permute-done.4.refs_1_ = bf16[4,32,128,128]{3,2,1,0:T(8,128)(2,1)S(1)} collective-permute-done((bf16[4,32,128,128]{3,2,1,0:T(8,128)(2,1)}, bf16[4,32,128,128]{3,2,1,0:T(8,128)(2,1)S(1)}, u32[]{:S(2)}, u32[]{:S(2)}) %collective-permute-start.4) | collective-permute-done | bytes 4194336 | tf_op jit(solution)/shard_map/ppermute | solution.py:313
  342.1 2.0 copy-done.10
  344.1 2.2 copy-done.4
  346.3 9.1 %shard_map.86.part = bf16[256,6144]{1,0:T(8,128)(2,1)S(1)} custom-call(s32[1]{0:T(128)} %bitcast.14.active, s32[512]{0:T(512)S(1)} %constant_dynamic-update-slice_fusion.slots, s32[8]{0:T(128)S(1)} %pad_add_fusion.counts, bf16[48,256,128]{2,1,0:T(8,128)(2,1)S(1)} %shard_map.85.hidden, bf16[4,32,128,128]{3,2,1,0:T(8,128)(2,1)S(1)} %bitcast.30, ...), custom_call_target="tpu_custom_call" | custom-call | flops 2147483648 | bytes 8388608 | tf_op jit(solution)/shard_map/pallas_call | solution.py:138
  355.5 22.0 %shard_map.87 = bf16[256,1536]{1,0:T(8,128)(2,1)S(1)} custom-call(bf16[256,6144]{1,0:T(8,128)(2,1)S(1)} %shard_map.86.part, bf16[256,1536]{1,0:T(8,128)(2,1)S(1)} %constant_dynamic-slice_fusion.current), custom_call_target="tpu_custom_call" | custom-call | flops 1572864 | bytes 25165824 | tf_op jit(solution)/shard_map/pallas_call | solution.py:247
  (50 shorter events, 11.3 us)
Async XLA Ops:
  6.5 161.3 %all-gather.8.cloned.1.call-start = ((), (), s32[]{:S(2)}) async-start(), calls=%async_computation | async-start | bytes 10485760 | tf_op jit(solution)/shard_map/all_gather | solution.py:277
  6.5 6.3 %collective-permute-start.1 = (bf16[64,128,128]{2,1,0:T(8,128)(2,1)}, bf16[64,128,128]{2,1,0:T(8,128)(2,1)S(1)}, u32[]{:S(2)}, u32[]{:S(2)}) collective-permute-start(bf16[64,128,128]{2,1,0:T(8,128)(2,1)} %bitcast.33), channel_id=1, source_target_pairs={{0,16},{1,17},{2,18},{3,19},{4,20},{5,21},{6,22},{7,23},{8,24},{9,... | collective-permute-start | bytes 6291464 | tf_op jit(solution)/shard_map/ppermute | solution.py:275
  16.0 1.9 copy-start.9
  16.0 236.0 %all-gather.10.cloned.1.call-start = ((), (), s32[]{:S(2)}) async-start(), calls=%async_computation.1 | async-start | bytes 5242880 | tf_op jit(solution)/shard_map/all_gather | solution.py:290
  18.0 6.2 %copy-start.13 = (u32[32]{0:T(128)S(1)}, u32[32]{0:T(128)}, u32[]{:S(2)}) copy-start(u32[32]{0:T(128)} %constant.27) | copy-start | bytes 388
  18.0 7.5 %copy-start.11 = (s32[1,1,1,64]{3,2,1,0:T(1,128)S(1)}, s32[1,1,1,64]{3,2,1,0:T(1,128)}, u32[]{:S(2)}) copy-start(s32[1,1,1,64]{3,2,1,0:T(1,128)} %param.14) | copy-start | bytes 772
  18.0 7.5 %copy-start.12 = (s32[1,1,1,64]{3,2,1,0:T(1,128)S(1)}, s32[1,1,1,64]{3,2,1,0:T(1,128)}, u32[]{:S(2)}) copy-start(s32[1,1,1,64]{3,2,1,0:T(1,128)} %param.11) | copy-start | bytes 772
  19.5 18.5 %collective-permute-start = (bf16[64,128,128]{2,1,0:T(8,128)(2,1)}, bf16[64,128,128]{2,1,0:T(8,128)(2,1)}, u32[]{:S(2)}, u32[]{:S(2)}) collective-permute-start(bf16[64,128,128]{2,1,0:T(8,128)(2,1)} %pad_maximum_fusion), channel_id=1, source_target_pairs={{16,0},{17,1},{18,2},{19,3},{20,4},{21,5},{22,6},{23,7},{24,8},{25... | collective-permute-start | bytes 6291464 | tf_op jit(solution)/shard_map/ppermute | solution.py:276
  38.0 135.4 %copy-start = (bf16[2,128,6144]{2,1,0:T(8,128)(2,1)S(1)}, bf16[2,128,6144]{2,1,0:T(8,128)(2,1)}, u32[]{:S(2)}) copy-start(bf16[2,128,6144]{2,1,0:T(8,128)(2,1)} %param.8) | copy-start | bytes 9437188
  41.9 133.0 %copy-start.8 = (f32[1,6144]{1,0:T(1,128)S(1)}, f32[1,6144]{1,0:T(1,128)}, u32[]{:S(2)}) copy-start(f32[1,6144]{1,0:T(1,128)} %gain.3) | copy-start | bytes 73732
  167.8 15.5 %collective-permute-start.2 = (bf16[4,64,128,128]{3,2,1,0:T(8,128)(2,1)}, bf16[4,64,128,128]{3,2,1,0:T(8,128)(2,1)}, u32[]{:S(2)}, u32[]{:S(2)}) collective-permute-start(bf16[4,64,128,128]{3,2,1,0:T(8,128)(2,1)} %bitcast.31), channel_id=1, source_target_pairs={{16,0},{17,1},{18,2},{19,3},{20,4},{21,5},{22,6},{23,7},{24,8},{25... | collective-permute-start | bytes 25165832 | tf_op jit(solution)/shard_map/ppermute | solution.py:301
  173.4 159.5 %all-gather.12.cloned.1.call-start = ((), (), s32[]{:S(2)}) async-start(), calls=%async_computation.2 | async-start | bytes 5242880 | tf_op jit(solution)/shard_map/all_gather | solution.py:307
  178.5 8.2 %copy-start.5 = (bf16[256,1536]{1,0:T(8,128)(2,1)S(1)}, bf16[256,1536]{1,0:T(8,128)(2,1)}, u32[]{:S(2)}) copy-start(bf16[256,1536]{1,0:T(8,128)(2,1)} %constant_dynamic-slice_fusion.1.current) | copy-start | bytes 2359300
  240.6 1.7 copy-start.1
  242.3 0.9 copy-start.6
  252.0 9.4 %collective-permute-start.3 = (bf16[4,32,128,128]{3,2,1,0:T(8,128)(2,1)}, bf16[4,32,128,128]{3,2,1,0:T(8,128)(2,1)}, u32[]{:S(2)}, u32[]{:S(2)}) collective-permute-start(bf16[4,32,128,128]{3,2,1,0:T(8,128)(2,1)} %bitcast.27), channel_id=1, source_target_pairs={{0,16},{1,17},{2,18},{3,19},{4,20},{5,21},{6,22},{7,23},{8,24},{9,... | collective-permute-start | bytes 12582920 | tf_op jit(solution)/shard_map/ppermute | solution.py:310
  261.4 2.2 copy-start.2
  263.6 2.2 copy-start.3
  332.9 9.3 %collective-permute-start.4 = (bf16[4,32,128,128]{3,2,1,0:T(8,128)(2,1)}, bf16[4,32,128,128]{3,2,1,0:T(8,128)(2,1)S(1)}, u32[]{:S(2)}, u32[]{:S(2)}) collective-permute-start(bf16[4,32,128,128]{3,2,1,0:T(8,128)(2,1)} %bitcast.29), channel_id=1, source_target_pairs={{0,16},{1,17},{2,18},{3,19},{4,20},{5,21},{6,22},{7,23},{8,24},{9,... | collective-permute-start | bytes 12582920 | tf_op jit(solution)/shard_map/ppermute | solution.py:313
  342.1 2.0 copy-start.10
  344.1 2.2 copy-start.4
  355.5 22.0 %copy-start.7 = (bf16[256,1536]{1,0:T(8,128)(2,1)S(1)}, bf16[256,1536]{1,0:T(8,128)(2,1)}, u32[]{:S(2)}) copy-start(bf16[256,1536]{1,0:T(8,128)(2,1)} %copy-done.6) | copy-start | bytes 2359300
Sparse Core Ops, SparseCore 0:
  16.1 151.6 all-gather.7
  173.5 78.4 all-gather.9
  253.6 79.2 all-gather.11
